TPU v7x, 512 devices: a whole 4x8x8 slice. The times are simulated.
512 devices in a mesh: comp: 8 (over x, y_hi), row: 64 (over z, y_lo, core).
Axes of the slice: x: 4, y: 8 (y_hi: 2, y_lo: 4; y = y_hi * 4 + y_lo), z: 8, core: 2. Of those that a mesh axis runs over, the one named last changes fastest.
Arguments:
- features: float32 [8, 16, 32768], P('comp', None, 'row'), may hold values from -6 to 6
- lengthscale: float32 [8, 16], P('comp'), may hold values from 1 to 3
- amplitude: float32 [8], P('comp'), may hold values from 0.5 to 2
- noise: float32 [1], replicated, may hold values from 0.5 to 2
- solution: float32 [128, 32768], P(None, 'row'), may hold values from -6 to 6
- residual: float32 [128, 32768], P(None, 'row'), may hold values from -12 to 12
- direction: float32 [128, 32768], P(None, 'row'), may hold values from -6 to 6
Outputs:
- new_solution: float32 [128, 32768], P(None, 'row')
- new_residual: float32 [128, 32768], P(None, 'row')
- new_direction: float32 [128, 32768], P(None, 'row')
All inputs are finite; a program needn't handle non-finite values.
Results may differ from a plain program's by a relative error of at most 0.017.
Values may be sent and summed in bfloat16 or wider, within the bound.
No kernel may reach another device: no remote copies, remote signals or barrier semaphores. Data moves between devices by JAX's collectives and lax.ppermute only.
A program may use at most 64 MiB of HBM per device.

v0:
```python
import math

import jax
import jax.numpy as jnp
from jax import lax
from jax.sharding import PartitionSpec as P


def kernel_terms(total, feats, dirs, scaled, sq_own, scale_amp):
    length = feats.shape[1]
    block = math.gcd(length, 512)
    count = length // block

    def step(index, acc):
        begin = index * block
        feat_block = lax.dynamic_slice_in_dim(feats, begin, block, 1)
        dir_block = lax.dynamic_slice_in_dim(dirs, begin, block, 1)
        wide = feat_block.astype(jnp.float32)
        sq_far = jnp.sum(wide * wide, axis=0)
        cross = jnp.einsum("fj,fi->ji", feat_block, scaled, preferred_element_type=jnp.float32)
        dist = sq_far[:, None] + sq_own[None, :] - 2.0 * cross
        weight = (scale_amp * jnp.exp(-0.5 * dist)).astype(jnp.bfloat16)
        return acc + jnp.dot(dir_block, weight, preferred_element_type=jnp.float32)

    return lax.fori_loop(0, count, step, total)


def cg_update(solution, residual, direction, image):
    own_norm = jnp.sum(residual * residual, axis=1)
    own_curve = jnp.sum(direction * image, axis=1)
    norm_now = lax.psum(own_norm, "row")
    curve = lax.psum(own_curve, "row")
    alpha = norm_now / curve
    new_solution = solution + alpha[:, None] * direction
    new_residual = residual - alpha[:, None] * image
    fresh = lax.psum(jnp.sum(new_residual * new_residual, axis=1), "row")
    new_direction = new_residual + (fresh / norm_now)[:, None] * direction
    return (new_solution, new_residual, new_direction)


def local(features, lengthscale, amplitude, noise, solution, residual, direction):
    scaled = (features[0] / lengthscale[0][:, None]).astype(jnp.bfloat16)
    wide_own = scaled.astype(jnp.float32)
    sq_own = jnp.sum(wide_own * wide_own, axis=0)
    scale_amp = amplitude[0]
    dir_low = direction.astype(jnp.bfloat16)
    probes = direction.shape[0]
    empty = jnp.zeros((probes, scaled.shape[1]), jnp.float32)
    partial_value = kernel_terms(
        empty,
        lax.all_gather(scaled, "row", axis=1, tiled=True),
        lax.all_gather(dir_low, "row", axis=1, tiled=True),
        scaled,
        sq_own,
        scale_amp,
    )
    image = lax.psum(partial_value, "comp") + noise[0] * direction
    return cg_update(solution, residual, direction, image)


def solution(mesh):
    in_specs = (
        P("comp", None, "row"),
        P("comp", None),
        P("comp"),
        P(),
        P(None, "row"),
        P(None, "row"),
        P(None, "row"),
    )
    out_specs = (P(None, "row"), P(None, "row"), P(None, "row"))
    return jax.shard_map(local, mesh=mesh, in_specs=in_specs, out_specs=out_specs, check_vma=False)
```

profile of v0, /device:TPU:1, one launch (start us, length us, event | category | flops | bytes accessed | tf_op | source)
XLA Modules:
  0.0 839.6 jit_solution(5921926541238870477)
XLA Ops:
  10.5 121.9 %all-gather.5.cloned.1.call-done = bf16[16,32768]{1,0:T(8,128)(2,1)} async-done(((bf16[16,512]{1,0:T(8,128)(2,1)}), bf16[16,32768]{1,0:T(8,128)(2,1)}) %all-gather.5.cloned.1.call-update) | async-done | bytes 1048592 | tf_op jit(solution)/shard_map/all_gather | solution.py:51
  132.4 125.2 %all-gather.3.cloned.1.call-done = bf16[128,32768]{1,0:T(8,128)(2,1)} async-done(((bf16[128,512]{1,0:T(8,128)(2,1)}), bf16[128,32768]{1,0:T(8,128)(2,1)}) %all-gather.3.cloned.1.call-update) | async-done | bytes 8388624 | tf_op jit(solution)/shard_map/all_gather | solution.py:52
  257.7 192.3 %while.14 = (s32[]{:T(128)}, f32[128,512]{1,0:T(8,128)S(1)}, bf16[128,32768]{1,0:T(8,128)(2,1)}, f32[]{:T(128)}, bf16[16,32768]{1,0:T(8,128)(2,1)}, /*index=5*/f...) while((s32[]{:T(128)}, f32[128,512]{1,0:T(8,128)S(1)}, ...), condition=%wide.region_5.0_spmd.clone, body=%wide.region_3.5_spmd.clone.sunk | while | flops 77225480 | bytes 712872 | solution.py:25
  258.4 2.2 fusion.30
  261.4 2.2 fusion.30
  264.4 2.2 fusion.30
  267.4 2.2 fusion.30
  270.4 2.2 fusion.30
  273.4 2.2 fusion.30
  279.4 2.2 fusion.30
  282.4 2.2 fusion.30
  285.4 2.2 fusion.30
  288.4 2.2 fusion.30
  294.4 2.2 fusion.30
  297.5 2.2 fusion.30
  300.5 2.2 fusion.30
  303.5 2.2 fusion.30
  306.5 2.2 fusion.30
  309.5 2.2 fusion.30
  312.5 2.2 fusion.30
  315.5 2.2 fusion.30
  318.5 2.2 fusion.30
  321.5 2.2 fusion.30
  324.5 2.2 fusion.30
  327.5 2.2 fusion.30
  330.5 2.2 fusion.30
  333.5 2.2 fusion.30
  336.5 2.2 fusion.30
  339.5 2.2 fusion.30
  342.5 2.2 fusion.30
  345.5 2.2 fusion.30
  348.5 2.2 fusion.30
  351.5 2.2 fusion.30
  354.5 2.2 fusion.30
  357.5 2.2 fusion.30
  360.6 2.2 fusion.30
  363.6 2.2 fusion.30
  366.6 2.2 fusion.30
  369.6 2.2 fusion.30
  372.6 2.2 fusion.30
  375.6 2.2 fusion.30
  378.6 2.2 fusion.30
  381.6 2.2 fusion.30
  387.6 2.2 fusion.30
  390.6 2.2 fusion.30
  393.6 2.2 fusion.30
  396.6 2.2 fusion.30
  402.6 2.2 fusion.30
  405.6 2.2 fusion.30
  408.6 2.2 fusion.30
  411.6 2.2 fusion.30
  417.6 2.2 fusion.30
  420.6 2.2 fusion.30
  423.7 2.2 fusion.30
  426.7 2.2 fusion.30
  429.7 2.2 fusion.30
  432.7 2.2 fusion.30
  435.7 2.2 fusion.30
  438.7 2.2 fusion.30
  444.7 2.2 fusion.30
  447.7 2.2 fusion.30
  451.4 105.5 %all-reduce.3.cloned.1.call-done = f32[128,512]{1,0:T(8,128)} async-done(((f32[128,512]{1,0:T(8,128)}), f32[128,512]{1,0:T(8,128)}) %all-reduce.3.cloned.1.call-update) | async-done | bytes 262160 | tf_op jit(solution)/shard_map/psum | solution.py:57
  558.1 138.9 %all-reduce = (f32[128]{0:T(128)S(1)}, f32[128]{0:T(128)S(1)}) all-reduce(f32[128]{0:T(128)S(1)} %multiply_reduce_fusion.3, f32[128]{0:T(128)S(1)} %multiply_reduce_fusion.2), channel_id=1, replica_groups=mesh['comp'=8,'row'=64] {'row'}, use_global_device_ids=true, to_apply=%region_1.2 | all-reduce | flops 256 | bytes 2048 | tf_op jit(solution)/shard_map/psum | solution.py:31
  698.8 133.5 %psum.31 = f32[128]{0:T(128)S(1)} all-reduce(f32[128]{0:T(128)S(1)} %get-tuple-element.168), channel_id=1, replica_groups=mesh['comp'=8,'row'=64] {'row'}, use_global_device_ids=true, to_apply=%region_10.0 | all-reduce | flops 128 | bytes 1024 | tf_op jit(solution)/shard_map/psum | solution.py:36
  (95 shorter events, 68.7 us)
Async XLA Ops:
  7.2 549.8 %copy-start = (f32[128,512]{1,0:T(8,128)S(1)}, f32[128,512]{1,0:T(8,128)}, u32[]{:S(2)}) copy-start(f32[128,512]{1,0:T(8,128)} %param.15) | copy-start | bytes 786436
  7.2 444.1 %copy-start.1 = (f32[128,512]{1,0:T(8,128)S(1)}, f32[128,512]{1,0:T(8,128)}, u32[]{:S(2)}) copy-start(f32[128,512]{1,0:T(8,128)} %param.14) | copy-start | bytes 786436
  7.2 689.8 %copy-start.3 = (f32[128,512]{1,0:T(8,128)S(1)}, f32[128,512]{1,0:T(8,128)}, u32[]{:S(2)}) copy-start(f32[128,512]{1,0:T(8,128)} %param.13) | copy-start | bytes 786436
  7.2 125.2 %all-gather.5.cloned.1.call-start = ((), (), s32[]{:S(2)}) async-start(), calls=%async_computation.1 | async-start | bytes 1064960 | tf_op jit(solution)/shard_map/all_gather | solution.py:51
  8.8 248.9 %all-gather.3.cloned.1.call-start = ((), (), s32[]{:S(2)}) async-start(), calls=%async_computation | async-start | bytes 8519680 | tf_op jit(solution)/shard_map/all_gather | solution.py:52
  10.5 546.5 %all-reduce.3.cloned.1.call-start = ((), (), s32[]{:S(2)}) async-start(), calls=%async_computation.2 | async-start | bytes 524288 | tf_op jit(solution)/shard_map/psum | solution.py:57
  449.9 0.7 copy-start.4
  698.8 134.3 %copy-start.2 = (f32[128,512]{1,0:T(8,128)}, f32[128,512]{1,0:T(8,128)S(1)}, u32[]{:S(2)}) copy-start(f32[128,512]{1,0:T(8,128)S(1)} %get-tuple-element.169) | copy-start | bytes 786436
Sparse Core Ops, SparseCore 0:
  10.8 121.5 all-gather.4
  135.1 122.4 all-gather.2
  450.8 106.1 all-reduce.2
where the time goes:
time: 845 us; the launch traced here: 840 us
  waiting for transfers between devices  353 us (42%)
  blocking collectives  272 us (32%)
  matrix products  143 us (17%)
  other arithmetic  54.4 us (6%)
  between operations  14.5 us (2%)
    dot_general x64, matrix products, step(): return acc + jnp.dot(dir_block, weight, preferred_element_type=jnp.float32)  143 us
    psum x1, blocking collectives, cg_update(): norm_now = lax.psum(own_norm, 'row')  139 us
    psum x1, blocking collectives, cg_update(): fresh = lax.psum(jnp.sum(new_residual * new_residual, axis=1), 'row')  134 us
    all_gather x1, waiting for transfers between devices, local(): lax.all_gather(dir_low, 'row', axis=1, tiled=True)  125 us
    all_gather x1, waiting for transfers between devices, local(): lax.all_gather(scaled, 'row', axis=1, tiled=True)  122 us
    psum x1, waiting for transfers between devices, local(): image = lax.psum(partial_value, 'comp') + noise[0] * direction  106 us
    reduce_sum x64, other arithmetic, step(): sq_far = jnp.sum(wide * wide, axis=0)  47.5 us
  transfers between devices with their start and end apart: 3, of which 3 were waited for; matrix products, arithmetic and copies ran while one was open for 0% of the time, Pallas kernels for 0%

commit v1 on v0

v1 whole, which is shorter than its diff:
```python
import jax
import jax.numpy as jnp
from jax import lax
from jax.experimental import pallas as pl
from jax.experimental.pallas import tpu as pltpu
from jax.sharding import Mesh, PartitionSpec as P

COMPS = 8
FEAT = 16
PROBES = 128
OWN = 512
SUB = OWN // COMPS
BLOCK = 1024
NAMES = ("x", "h", "z", "y", "k")
SIZES = (4, 2, 8, 4, 2)

bf16 = jnp.bfloat16
f32 = jnp.float32


def split3(value):
    first = value.astype(bf16)
    rest = value - first.astype(f32)
    second = rest.astype(bf16)
    rest = rest - second.astype(f32)
    return first, second, rest.astype(bf16)


def dot(a, b):
    return jnp.dot(a, b, preferred_element_type=f32)


def weights_kernel(far_ref, own_ref, out_ref, lhs, dirs, rhs):
    points = far_ref.shape[0] * SUB
    lane = lax.broadcasted_iota(jnp.int32, (128, 128), 1)
    row = lax.broadcasted_iota(jnp.int32, (128, 128), 0)
    group = jnp.where((row // FEAT == lane % 8) & (lane < 24), 1.0, 0.0).astype(bf16)
    spot = lax.broadcasted_iota(jnp.int32, (256, 128), 1)

    @pl.loop(0, points // 256)
    def _(index):
        piece = far_ref[pl.ds(index * 4, 4)]
        far_dirs = piece[:, 0].reshape(256, 128)
        feats = piece[:, 1].reshape(256, 128)
        wide = feats.astype(f32)
        square = wide * wide
        high = square.astype(bf16)
        low = (square - high.astype(f32)).astype(bf16)
        half = -0.5 * (dot(high, group) + dot(low, group))
        a0, a1, a2 = (term.astype(f32) for term in split3(half))
        aux = jnp.where(spot < 8, a0, jnp.where(spot < 16, a1, jnp.where(spot < 24, a2, jnp.where(spot < 27, 1.0, 0.0))))
        rows = pl.ds(pl.multiple_of(index * 256, 256), 256)
        lhs[rows, :128] = feats
        lhs[rows, 128:] = aux.astype(bf16)
        dirs[:, rows] = far_dirs.T

    own = own_ref[...]
    feats = own[:, :, :OWN].reshape(128, OWN).astype(f32)
    line = lax.broadcasted_iota(jnp.int32, (128, OWN), 0)
    for c in range(COMPS):
        mine = own[c, :, :OWN].astype(f32)
        log_amp = jnp.sum(own[c, :, OWN:].astype(f32), axis=0, keepdims=True)[:, :1]
        offset = log_amp - 0.5 * jnp.sum(mine * mine, axis=0, keepdims=True)
        b0, b1, b2 = (jnp.broadcast_to(term.astype(f32), (128, OWN)) for term in split3(offset))
        rhs[c, :128] = jnp.where(line // FEAT == c, feats, 0.0).astype(bf16)
        tail = jnp.where(line == 24, b0, jnp.where(line == 25, b1, jnp.where(line == 26, b2, 0.0)))
        rhs[c, 128:] = jnp.where((line < 24) & (line % 8 == c), 1.0, tail).astype(bf16)

    out_ref[...] = jnp.zeros_like(out_ref)

    @pl.loop(0, points // BLOCK)
    def _(index):
        rows = pl.ds(pl.multiple_of(index * BLOCK, BLOCK), BLOCK)
        left = lhs[rows, :]
        far_dirs = dirs[:, rows]
        total = jnp.zeros((PROBES, OWN), f32)
        for c in range(COMPS):
            weight = jnp.exp(dot(left, rhs[c])).astype(bf16)
            total = total + dot(far_dirs, weight)
        out_ref[...] += total


def kernel_terms(far, own):
    points = far.shape[0] * SUB
    return pl.pallas_call(
        weights_kernel,
        out_shape=jax.ShapeDtypeStruct((PROBES, OWN), f32),
        in_specs=[pl.BlockSpec(memory_space=pltpu.VMEM)] * 2,
        out_specs=pl.BlockSpec(memory_space=pltpu.VMEM),
        scratch_shapes=[
            pltpu.VMEM((points, 256), bf16),
            pltpu.VMEM((PROBES, points), bf16),
            pltpu.VMEM((COMPS, 256, OWN), bf16),
        ],
        compiler_params=pltpu.CompilerParams(vmem_limit_bytes=48 << 20),
        cost_estimate=pl.CostEstimate(
            flops=2 * points * OWN * COMPS * 384,
            bytes_accessed=points * 512,
            transcendentals=points * OWN * COMPS,
        ),
    )(far, own)


def spread(value, axes, count):
    return lax.all_to_all(jnp.broadcast_to(value[None], (count,) + value.shape), axes, 0, 0, tiled=True)


def local(features, lengthscale, amplitude, noise, solution, residual, direction):
    comp = lax.axis_index("x") * 2 + lax.axis_index("h")
    scaled = (features[0] / lengthscale[0][:, None]).astype(bf16)
    log_amp = split3(jnp.log(amplitude))
    extra = jnp.concatenate(log_amp + (jnp.zeros((FEAT - 3,), bf16),))
    extra = jnp.broadcast_to(extra[:, None], (FEAT, 128))
    own = spread(jnp.concatenate((scaled, extra), axis=1), ("x", "h"), COMPS)

    feats = own[:, :, :OWN].reshape(COMPS * FEAT, OWN)
    both = jnp.stack((direction.astype(bf16).T, feats.T))
    piece = lax.dynamic_slice_in_dim(both, comp * SUB, SUB, 1)
    far = spread(piece, ("z", "y"), 32)
    far = lax.all_gather(far, "k", axis=0, tiled=True)

    part = kernel_terms(far, own)
    parts = spread(part.astype(bf16), ("x", "h"), COMPS)
    image = jnp.sum(parts.astype(f32), axis=0) + noise[0] * direction

    sums = jnp.stack(
        (
            jnp.sum(residual * residual, axis=1),
            jnp.sum(direction * image, axis=1),
            jnp.sum(residual * image, axis=1),
            jnp.sum(image * image, axis=1),
        )
    )
    sums = jnp.sum(spread(sums, ("z", "y", "k"), 64), axis=0)
    norm_now, curve, mixed, image_norm = sums[0], sums[1], sums[2], sums[3]
    alpha = norm_now / curve
    fresh = jnp.maximum(norm_now + alpha * (alpha * image_norm - 2.0 * mixed), 0.0)
    beta = fresh / norm_now
    new_solution = solution + alpha[:, None] * direction
    new_residual = residual - alpha[:, None] * image
    new_direction = new_residual + beta[:, None] * direction
    return new_solution, new_residual, new_direction


def solution(mesh):
    fine = Mesh(mesh.devices.reshape(SIZES), NAMES)
    comp, row = ("x", "h"), ("z", "y", "k")
    in_specs = (
        P(comp, None, row),
        P(comp, None),
        P(comp),
        P(),
        P(None, row),
        P(None, row),
        P(None, row),
    )
    out_specs = (P(None, row), P(None, row), P(None, row))
    return jax.shard_map(local, mesh=fine, in_specs=in_specs, out_specs=out_specs, check_vma=False)
```

time: 845 us -> 172 us (0.20)
  waiting for transfers between devices: 353 us -> 48.5 us
  blocking collectives: 272 us -> 63.8 us
  matrix products: 143 us -> 0 us
  other arithmetic: 54.4 us -> 3.45 us
  Pallas kernels: 0 us -> 18.2 us
  starting transfers between devices: 0.12 us -> 18.2 us
    psum x2 -> x0, blocking collectives: 272 us -> none  [the longest x1 139 us: cg_update(): norm_now = lax.psum(own_norm, 'row')]
    all_gather x2 -> x1, waiting for transfers between devices: 247 us -> 15 us  [local(): far = lax.all_gather(far, 'k', axis=0, tiled=True)]
    dot_general x64 -> x0, matrix products: 143 us -> none  [step(): return acc + jnp.dot(dir_block, weight, preferred_element_type=jnp.float32)]
    psum x1 -> x0, waiting for transfers between devices: 106 us -> none  [local(): image = lax.psum(partial_value, 'comp') + noise[0] * direction]
    all_to_all x0 -> x2, blocking collectives: none -> 63.8 us  [spread(): lax.all_to_all(jnp.broadcast_to(value[None], (count,) + value.shape), axe...]
    reduce_sum x68 -> x3, other arithmetic: 52 us -> 0.4 us  [the longest x1 0.18 us: local(): jnp.sum(residual * residual, axis=1)]
    all_to_all x0 -> x2, waiting for transfers between devices: none -> 33.5 us  [spread(): lax.all_to_all(jnp.broadcast_to(value[None], (count,) + value.shape), axe...]
    pallas_call x0 -> x1, Pallas kernels: none -> 18.2 us  [kernel_terms(): pl.pallas_call(weights_kernel, out_shape=jax.ShapeDtypeStruct((PROBES, OW...]
  transfers between devices with their start and end apart: 3 -> 3, of which waited for: 3 -> 3; matrix products, arithmetic and copies ran while one was open for 0% -> 1% of each run, Pallas kernels for 0% -> 0%
where the time goes in v1:
time: 172 us; the launch traced here: 171 us
  blocking collectives  63.8 us (37%)
  waiting for transfers between devices  48.5 us (28%)
  starting transfers between devices  18.2 us (11%)
  Pallas kernels  18.2 us (11%)
  between operations  15.5 us (9%)
  local copies, waits for them, and re-layouts  3.82 us (2%)
  other arithmetic  3.45 us (2%)
    all_to_all x2, blocking collectives, spread(): lax.all_to_all(jnp.broadcast_to(value[None], (count,) + value.shape), axe...  63.8 us
    all_to_all x2, waiting for transfers between devices, spread(): lax.all_to_all(jnp.broadcast_to(value[None], (count,) + value.shape), axe...  33.5 us
    pallas_call x1, Pallas kernels, kernel_terms(): pl.pallas_call(weights_kernel, out_shape=jax.ShapeDtypeStruct((PROBES, OW...  18.2 us
    all_to_all x2, starting transfers between devices, spread(): lax.all_to_all(jnp.broadcast_to(value[None], (count,) + value.shape), axe...  18.1 us
    all_gather x1, waiting for transfers between devices, local(): far = lax.all_gather(far, 'k', axis=0, tiled=True)  15 us
  transfers between devices with their start and end apart: 3, of which 3 were waited for; matrix products, arithmetic and copies ran while one was open for 1% of the time, Pallas kernels for 0%

profile of v1, /device:TPU:1, one launch (start us, length us, event | category | flops | bytes accessed | tf_op | source)
XLA Modules:
  0.0 171.4 jit_solution(17855537747447354245)
XLA Ops:
  7.9 0.1 pad_maximum_fusion.2
  8.0 0.8 fusion.1
  8.8 0.1 broadcast_in_dim.10
  8.9 0.7 broadcast_in_dim.11
  9.6 10.1 %all-to-all-start = ((bf16[8,16,640]{2,1,0:T(8,128)(2,1)}), bf16[8,16,640]{2,1,0:T(8,128)(2,1)S(1)}, u32[]{:S(2)}, u32[]{:S(2)}) async-start(bf16[8,16,640]{2,1,0:T(8,128)(2,1)} %broadcast_in_dim.11), calls=%async_computation | async-start | bytes 327680 | tf_op jit(solution)/shard_map/all_to_all | solution.py:105
  19.7 0.0 all-gather.2.cloned.1.call-start
  19.7 1.0 convert_bitcast_fusion
  20.7 8.7 %all-to-all-done.own_ref = bf16[8,16,640]{2,1,0:T(8,128)(2,1)S(1)} async-done(((bf16[8,16,640]{2,1,0:T(8,128)(2,1)}), bf16[8,16,640]{2,1,0:T(8,128)(2,1)S(1)}, u32[]{:S(2)}, u32[]{:S(2)}) %all-to-all-start) | async-done | bytes 163872 | tf_op jit(solution)/shard_map/all_to_all | solution.py:105
  29.4 0.1 fusion
  29.5 0.1 copy.13
  29.6 0.2 broadcast_in_dim.12
  29.8 38.8 %all_to_all.20 = bf16[32,2,64,128]{3,2,1,0:T(8,128)(2,1)} all-to-all(bf16[32,2,64,128]{3,2,1,0:T(8,128)(2,1)S(1)} %broadcast_in_dim.12), channel_id=1, replica_groups=mesh['x'=4,'h'=2,'z'=8,'y'=4,'k'=2] {'z','y'}, dimensions={0} | all-to-all | bytes 2097152 | tf_op jit(solution)/shard_map/all_to_all | solution.py:105
  68.7 0.0 all-gather.2.cloned.1.call-update
  68.7 15.0 %all-gather.2.cloned.1.call-done.far_ref = bf16[64,2,64,128]{3,2,1,0:T(8,128)(2,1)} async-done(((bf16[32,2,64,128]{3,2,1,0:T(8,128)(2,1)}), bf16[64,2,64,128]{3,2,1,0:T(8,128)(2,1)}) %all-gather.2.cloned.1.call-update) | async-done | bytes 2097168 | tf_op jit(solution)/shard_map/all_gather | solution.py:120
  83.7 0.0 copy-start
  83.7 1.6 copy-done
  85.2 18.2 %shard_map.94 = f32[128,512]{1,0:T(8,128)S(1)} custom-call(bf16[64,2,64,128]{3,2,1,0:T(8,128)(2,1)S(1)} %copy-done, bf16[8,16,640]{2,1,0:T(8,128)(2,1)S(1)} %all-to-all-done.own_ref), custom_call_target="tpu_custom_call" | custom-call | flops 12884901888 | bytes 2097152 | tf_op jit(solution)/shard_map/pallas_call | solution.py:85
  103.5 0.0 copy-start.1
  103.5 0.0 copy-start.2
  103.5 1.1 broadcast_in_dim.13
  104.6 0.0 copy-start.3
  104.6 8.0 %all-to-all-start.2 = ((bf16[8,128,512]{2,1,0:T(8,128)(2,1)}), bf16[8,128,512]{2,1,0:T(8,128)(2,1)S(1)}, u32[]{:S(2)}, u32[]{:S(2)}) async-start(bf16[8,128,512]{2,1,0:T(8,128)(2,1)} %broadcast_in_dim.13), calls=%async_computation.2 | async-start | bytes 2097152 | tf_op jit(solution)/shard_map/all_to_all | solution.py:105
  113.3 24.8 %all-to-all-done.2 = bf16[8,128,512]{2,1,0:T(8,128)(2,1)S(1)} async-done(((bf16[8,128,512]{2,1,0:T(8,128)(2,1)}), bf16[8,128,512]{2,1,0:T(8,128)(2,1)S(1)}, u32[]{:S(2)}, u32[]{:S(2)}) %all-to-all-start.2) | async-done | bytes 1048608 | tf_op jit(solution)/shard_map/all_to_all | solution.py:105
  138.1 0.1 convert_reduce_fusion
  138.2 0.0 copy-done.1
  138.2 0.0 copy-done.2
  138.2 0.2 multiply_reduce_fusion.3
  138.5 24.9 %all_to_all.21 = f32[64,4,128]{2,1,0:T(4,128)S(1)} all-to-all(f32[64,4,128]{2,1,0:T(4,128)S(1)} %broadcast_in_dim.14), channel_id=1, replica_groups=mesh['x'=4,'h'=2,'z'=8,'y'=4,'k'=2] {'z','y','k'}, dimensions={0} | all-to-all | bytes 262144 | tf_op jit(solution)/shard_map/all_to_all | solution.py:105
  163.4 0.1 reduce_sum.59
  163.5 0.0 copy-done.3
  163.5 1.0 multiply_add_fusion
  (7 shorter events, 0.1 us)
Async XLA Ops:
  9.6 19.8 %all-to-all-start = ((bf16[8,16,640]{2,1,0:T(8,128)(2,1)}), bf16[8,16,640]{2,1,0:T(8,128)(2,1)S(1)}, u32[]{:S(2)}, u32[]{:S(2)}) async-start(bf16[8,16,640]{2,1,0:T(8,128)(2,1)} %broadcast_in_dim.11), calls=%async_computation | async-start | bytes 327680 | tf_op jit(solution)/shard_map/all_to_all | solution.py:105
  19.7 64.0 %all-gather.2.cloned.1.call-start = ((), (), s32[]{:S(2)}) async-start(), calls=%async_computation.4 | async-start | bytes 3145728 | tf_op jit(solution)/shard_map/all_gather | solution.py:120
  83.7 1.6 copy-start
  103.5 34.7 %copy-start.1 = (f32[128,512]{1,0:T(8,128)S(1)}, f32[128,512]{1,0:T(8,128)}, u32[]{:S(2)}) copy-start(f32[128,512]{1,0:T(8,128)} %param.13) | copy-start | bytes 786436
  103.5 34.7 %copy-start.2 = (f32[128,512]{1,0:T(8,128)S(1)}, f32[128,512]{1,0:T(8,128)}, u32[]{:S(2)}) copy-start(f32[128,512]{1,0:T(8,128)} %param.12) | copy-start | bytes 786436
  104.6 58.9 %copy-start.3 = (f32[128,512]{1,0:T(8,128)S(1)}, f32[128,512]{1,0:T(8,128)}, u32[]{:S(2)}) copy-start(f32[128,512]{1,0:T(8,128)} %param.11) | copy-start | bytes 786436
  104.6 33.5 %all-to-all-start.2 = ((bf16[8,128,512]{2,1,0:T(8,128)(2,1)}), bf16[8,128,512]{2,1,0:T(8,128)(2,1)S(1)}, u32[]{:S(2)}, u32[]{:S(2)}) async-start(bf16[8,128,512]{2,1,0:T(8,128)(2,1)} %broadcast_in_dim.13), calls=%async_computation.2 | async-start | bytes 2097152 | tf_op jit(solution)/shard_map/all_to_all | solution.py:105
Sparse Core Ops, SparseCore 0:
  68.8 14.7 all-gather.1

commit v2 on v1

v2 whole, which is shorter than its diff:
```python
import jax
import jax.numpy as jnp
from jax import lax
from jax.experimental import pallas as pl
from jax.experimental.pallas import tpu as pltpu
from jax.sharding import Mesh, PartitionSpec as P

COMPS = 8
FEAT = 16
PROBES = 128
OWN = 512
SUB = OWN // COMPS
BLOCK = 1024
NAMES = ("x", "h", "z", "y", "k")
SIZES = (4, 2, 8, 4, 2)
PLANE = SIZES[2] * SIZES[3]
ROWS = PLANE * SIZES[4]

bf16 = jnp.bfloat16
f32 = jnp.float32
VMEM = pl.BlockSpec(memory_space=pltpu.VMEM)
SMEM = pl.BlockSpec(memory_space=pltpu.SMEM)


def split3(value):
    first = value.astype(bf16)
    rest = value - first.astype(f32)
    second = rest.astype(bf16)
    rest = rest - second.astype(f32)
    return first, second, rest.astype(bf16)


def dot(a, b):
    return jnp.dot(a, b, preferred_element_type=f32)


def call(kernel, outs, in_specs, args, scratch=(), cost=None):
    return pl.pallas_call(
        kernel,
        out_shape=tuple(jax.ShapeDtypeStruct(shape, dtype) for shape, dtype in outs),
        in_specs=in_specs,
        out_specs=(VMEM,) * len(outs),
        scratch_shapes=scratch,
        compiler_params=pltpu.CompilerParams(vmem_limit_bytes=40 << 20),
        cost_estimate=cost,
    )(*args)


def scale_kernel(features_ref, length_ref, amplitude_ref, out_ref, features, length, amplitude, sems):
    copies = [
        pltpu.make_async_copy(features_ref, features, sems.at[0]),
        pltpu.make_async_copy(length_ref, length, sems.at[1]),
        pltpu.make_async_copy(amplitude_ref, amplitude, sems.at[2]),
    ]
    for copy in copies:
        copy.start()
    for copy in copies:
        copy.wait()
    eye = lax.broadcasted_iota(jnp.int32, (FEAT, FEAT), 0) == lax.broadcasted_iota(jnp.int32, (FEAT, FEAT), 1)
    wide = jnp.sum(jnp.where(eye, length[...], 0.0), axis=1, keepdims=True)
    scaled = (features[0] / wide).astype(bf16)
    a0, a1, a2 = (term.astype(f32) for term in split3(jnp.log(jnp.full((FEAT, 128), amplitude[0], f32))))
    row = lax.broadcasted_iota(jnp.int32, (FEAT, 128), 0)
    extra = jnp.where(row == 0, a0, jnp.where(row == 1, a1, jnp.where(row == 2, a2, 0.0))).astype(bf16)
    for c in range(COMPS):
        out_ref[c, :, :OWN] = scaled
        out_ref[c, :, OWN:] = extra


def passing_kernel(begin_ref, own_ref, out_ref, turned):
    turned[...] = own_ref[:, :, :OWN].reshape(COMPS * FEAT, OWN).T
    piece = turned[pl.ds(pl.multiple_of(begin_ref[0], SUB), SUB), :]
    for index in range(PLANE):
        out_ref[index] = piece


def weights_kernel(far_ref, own_ref, mate_ref, dir_ref, mate_dir_ref, out_ref, lhs, dirs, rhs):
    line = lax.broadcasted_iota(jnp.int32, (128, OWN), 0)
    for side, (ref, side_dirs) in enumerate(((own_ref, dir_ref), (mate_ref, mate_dir_ref))):
        near = ref[...]
        columns = slice(side * OWN, (side + 1) * OWN)
        dirs[columns, :] = side_dirs[...].T
        feats = near[:, :, :OWN].reshape(128, OWN).astype(f32)
        for c in range(COMPS):
            mine = near[c, :, :OWN].astype(f32)
            log_amp = jnp.sum(near[c, :, OWN:].astype(f32), axis=0, keepdims=True)[:, :1]
            offset = log_amp - 0.5 * jnp.sum(mine * mine, axis=0, keepdims=True)
            b0, b1, b2 = (jnp.broadcast_to(term.astype(f32), (128, OWN)) for term in split3(offset))
            rhs[c, :128, columns] = jnp.where(line // FEAT == c, feats, 0.0).astype(bf16)
            tail = jnp.where(line == 24, b0, jnp.where(line == 25, b1, jnp.where(line == 26, b2, 0.0)))
            rhs[c, 128:, columns] = jnp.where((line < 24) & (line % 8 == c), 1.0, tail).astype(bf16)

    blocks = far_ref.shape[0]
    lane = lax.broadcasted_iota(jnp.int32, (128, 128), 1)
    row = lax.broadcasted_iota(jnp.int32, (128, 128), 0)
    group = jnp.where((row // FEAT == lane % 8) & (lane < 24), 1.0, 0.0).astype(bf16)
    spot = lax.broadcasted_iota(jnp.int32, (256, 128), 1)

    @pl.loop(0, blocks // 4)
    def _(index):
        feats = far_ref[pl.ds(index * 4, 4)].reshape(256, 128)
        wide = feats.astype(f32)
        square = wide * wide
        high = square.astype(bf16)
        low = (square - high.astype(f32)).astype(bf16)
        half = -0.5 * (dot(high, group) + dot(low, group))
        a0, a1, a2 = (term.astype(f32) for term in split3(half))
        aux = jnp.where(spot < 8, a0, jnp.where(spot < 16, a1, jnp.where(spot < 24, a2, jnp.where(spot < 27, 1.0, 0.0))))
        rows = pl.ds(pl.multiple_of(index * 256, 256), 256)
        lhs[rows, :128] = feats
        lhs[rows, 128:] = aux.astype(bf16)

    step = BLOCK // SUB
    for index in range(blocks // step):
        left = lhs[index * BLOCK : (index + 1) * BLOCK, :]
        weight = None
        for c in range(COMPS):
            term = jnp.exp(dot(left, rhs[c]))
            weight = term if weight is None else weight + term
        part = dot(weight.astype(bf16), dirs[...]).astype(bf16)
        out_ref[index * step : (index + 1) * step] = part.reshape(step, SUB, PROBES)


def add_kernel(parts_ref, out_ref):
    total = parts_ref[0].astype(f32)
    for index in range(1, PLANE):
        total = total + parts_ref[index].astype(f32)
    total = total.astype(bf16)
    for c in range(COMPS):
        out_ref[c] = total


def image_kernel(noise_ref, parts_ref, direction_ref, residual_ref, image_ref, sums_ref):
    direction = direction_ref[...]
    residual = residual_ref[...]
    image = parts_ref[...].reshape(OWN, PROBES).astype(f32).T + noise_ref[0] * direction
    image_ref[...] = image
    terms = (residual * residual, direction * image, residual * image, image * image)
    lane = lax.broadcasted_iota(jnp.int32, (PROBES, 8), 1)
    sums = jnp.zeros((PROBES, 8), f32)
    for index, term in enumerate(terms):
        sums = jnp.where(lane == index, jnp.sum(term, axis=1, keepdims=True), sums)
    sums = sums.T[:4]
    for index in range(ROWS):
        sums_ref[index] = sums


def update_kernel(sums_ref, image_ref, solution_ref, residual_ref, direction_ref, outs_ref, outr_ref, outd_ref):
    sums = sums_ref[0]
    for index in range(1, ROWS):
        sums = sums + sums_ref[index]
    norm_now, curve, mixed, image_norm = (sums[index : index + 1] for index in range(4))
    alpha = norm_now / curve
    fresh = jnp.maximum(norm_now + alpha * (alpha * image_norm - 2.0 * mixed), 0.0)
    beta = fresh / norm_now
    line = lax.broadcasted_iota(jnp.int32, (8, PROBES), 0)
    scalars = jnp.where(line == 0, alpha, jnp.where(line == 1, beta, 0.0)).T
    alpha, beta = scalars[:, :1], scalars[:, 1:2]
    direction = direction_ref[...]
    outs_ref[...] = solution_ref[...] + alpha * direction
    new_residual = residual_ref[...] - alpha * image_ref[...]
    outr_ref[...] = new_residual
    outd_ref[...] = new_residual + beta * direction


def swap(value):
    return lax.ppermute(value, "k", ((0, 1), (1, 0)))


def exchange(value, axes):
    return lax.all_to_all(value, axes, 0, 0, tiled=True)


def local(features, lengthscale, amplitude, noise, solution, residual, direction):
    low = direction.astype(bf16)
    mate_low = swap(low)
    (own,) = call(
        scale_kernel,
        (((COMPS, FEAT, OWN + 128), bf16),),
        (pl.BlockSpec(memory_space=pltpu.HBM),) * 3,
        (features, lengthscale, amplitude),
        (
            pltpu.VMEM((1, FEAT, OWN), f32),
            pltpu.VMEM((1, FEAT), f32),
            pltpu.SMEM((1,), f32),
            pltpu.SemaphoreType.DMA((3,)),
        ),
    )
    own = exchange(own, ("x", "h"))
    mate = swap(own)

    begin = ((lax.axis_index("x") * 2 + lax.axis_index("h")) * SUB).astype(jnp.int32)[None]
    far_shape = ((PLANE, SUB, PROBES), bf16)
    (far,) = call(passing_kernel, (far_shape,), (SMEM, VMEM), (begin, own), (pltpu.VMEM((OWN, COMPS * FEAT), bf16),))
    far = exchange(far, ("z", "y"))
    points = PLANE * SUB
    (part,) = call(
        weights_kernel,
        (far_shape,),
        (VMEM,) * 5,
        (far, own, mate, low, mate_low),
        (
            pltpu.VMEM((points, 256), bf16),
            pltpu.VMEM((2 * OWN, PROBES), bf16),
            pltpu.VMEM((COMPS, 256, 2 * OWN), bf16),
        ),
        pl.CostEstimate(
            flops=4 * points * OWN * (COMPS * 256 + 128), bytes_accessed=2 << 20, transcendentals=2 * points * OWN * COMPS
        ),
    )
    (part,) = call(add_kernel, (((COMPS, SUB, PROBES), bf16),), (VMEM,), (exchange(part, ("z", "y")),))
    image, sums = call(
        image_kernel,
        (((PROBES, OWN), f32), ((ROWS, 4, PROBES), f32)),
        (SMEM, VMEM, VMEM, VMEM),
        (noise, exchange(part, ("x", "h")), direction, residual),
    )
    sums = exchange(sums, ("z", "y", "k"))

    block = pl.BlockSpec((PROBES, OWN), lambda: (0, 0))
    return pl.pallas_call(
        update_kernel,
        out_shape=(jax.ShapeDtypeStruct((PROBES, OWN), f32),) * 3,
        in_specs=(VMEM,) * 5,
        out_specs=(block,) * 3,
        compiler_params=pltpu.CompilerParams(vmem_limit_bytes=40 << 20),
    )(sums, image, solution, residual, direction)


def solution(mesh):
    fine = Mesh(mesh.devices.reshape(SIZES), NAMES)
    comp, row = ("x", "h"), ("z", "y", "k")
    in_specs = (
        P(comp, None, row),
        P(comp, None),
        P(comp),
        P(),
        P(None, row),
        P(None, row),
        P(None, row),
    )
    out_specs = (P(None, row), P(None, row), P(None, row))
    return jax.shard_map(local, mesh=fine, in_specs=in_specs, out_specs=out_specs, check_vma=False)
```

time: 172 us -> 122 us (0.71)
  waiting for transfers between devices: 48.5 us -> 26.7 us
  blocking collectives: 63.8 us -> 42.7 us
  starting transfers between devices: 18.2 us -> 32.2 us
  between operations: 15.5 us -> 2.04 us
  other arithmetic: 3.45 us -> 0.02 us
  local copies, waits for them, and re-layouts: 3.82 us -> 0.77 us
    all_to_all x2, blocking collectives: 63.8 us -> 42.7 us  [exchange(): return lax.all_to_all(value, axes, 0, 0, tiled=True)]
    all_gather x1 -> x0, waiting for transfers between devices: 15 us -> none  [local(): far = lax.all_gather(far, 'k', axis=0, tiled=True)]
    all_to_all x2 -> x3, starting transfers between devices: 18.1 us -> 26.5 us  [exchange(): return lax.all_to_all(value, axes, 0, 0, tiled=True)]
    all_to_all x2 -> x3, waiting for transfers between devices: 33.5 us -> 25.3 us  [exchange(): return lax.all_to_all(value, axes, 0, 0, tiled=True)]
    ppermute x0 -> x2, starting transfers between devices: none -> 5.75 us  [swap(): return lax.ppermute(value, 'k', ((0, 1), (1, 0)))]
    broadcast_in_dim x5 -> x0, local copies, waits for them, and re-layouts: 2.1 us -> none  [the longest x4 2.03 us: spread(): jnp.broadcast_to(value[None], (count,) + value.shape)]
    pallas_call x1 -> x6, Pallas kernels: 18.2 us -> 17.4 us  [the longest x5 16.3 us: call(): pl.pallas_call(kernel, out_shape=tuple((jax.ShapeDtypeStruct(shape, dtype...]
  transfers between devices with their start and end apart: 3 -> 5, of which waited for: 3 -> 4; matrix products, arithmetic and copies ran while one was open for 1% -> 0% of each run, Pallas kernels for 0% -> 0%
where the time goes in v2:
time: 122 us
  blocking collectives  42.7 us (35%)
  starting transfers between devices  32.2 us (26%)
  waiting for transfers between devices  26.7 us (22%)
  Pallas kernels  17.4 us (14%)
  between operations  2.04 us (2%)
    all_to_all x2, blocking collectives, exchange(): return lax.all_to_all(value, axes, 0, 0, tiled=True)  42.7 us
    all_to_all x3, starting transfers between devices, exchange(): return lax.all_to_all(value, axes, 0, 0, tiled=True)  26.5 us
    all_to_all x3, waiting for transfers between devices, exchange(): return lax.all_to_all(value, axes, 0, 0, tiled=True)  25.3 us
    pallas_call x5, Pallas kernels, call(): pl.pallas_call(kernel, out_shape=tuple((jax.ShapeDtypeStruct(shape, dtype...  16.3 us
    ppermute x2, starting transfers between devices, swap(): return lax.ppermute(value, 'k', ((0, 1), (1, 0)))  5.75 us
  transfers between devices with their start and end apart: 5, of which 4 were waited for; matrix products, arithmetic and copies ran while one was open for 0% of the time, Pallas kernels for 0%

profile of v2, /device:TPU:1, one launch (start us, length us, event | category | flops | bytes accessed | tf_op | source)
XLA Modules:
  0.0 121.9 jit_solution(1984628069813995822)
XLA Ops:
  0.6 0.0 copy-start.4
  1.3 0.0 copy-done.4
  1.3 0.0 copy-start.3
  1.3 0.7 copy-done.3
  2.1 1.3 %shard_map.94 = bf16[8,16,640]{2,1,0:T(8,128)(2,1)} custom-call(f32[1,16,512]{2,1,0:T(8,128)S(1)} %copy-done.3, f32[1,16]{1,0:T(1,128)S(1)} %copy-done.4, f32[1]{0:T(128)S(6)} %copy.10.amplitude_ref), custom_call_target="tpu_custom_call" | custom-call | tf_op jit(solution)/shard_map/pallas_call | solution.py:38
  3.4 10.1 %all-to-all-start = ((bf16[8,16,640]{2,1,0:T(8,128)(2,1)}), bf16[8,16,640]{2,1,0:T(8,128)(2,1)S(1)}, u32[]{:S(2)}, u32[]{:S(2)}) async-start(bf16[8,16,640]{2,1,0:T(8,128)(2,1)} %shard_map.94), calls=%async_computation | async-start | bytes 327680 | tf_op jit(solution)/shard_map/all_to_all | solution.py:171
  13.5 9.7 %all-to-all-done.own_ref = bf16[8,16,640]{2,1,0:T(8,128)(2,1)S(1)} async-done(((bf16[8,16,640]{2,1,0:T(8,128)(2,1)}), bf16[8,16,640]{2,1,0:T(8,128)(2,1)S(1)}, u32[]{:S(2)}, u32[]{:S(2)}) %all-to-all-start) | async-done | bytes 163872 | tf_op jit(solution)/shard_map/all_to_all | solution.py:171
  23.2 1.0 shard_map.95
  24.2 0.0 copy-start
  24.2 12.8 %all-to-all-start.1 = ((bf16[32,64,128]{2,1,0:T(8,128)(2,1)}), bf16[32,64,128]{2,1,0:T(8,128)(2,1)S(1)}, u32[]{:S(2)}, u32[]{:S(2)}) async-start(bf16[32,64,128]{2,1,0:T(8,128)(2,1)} %shard_map.95), calls=%async_computation.1 | async-start | bytes 1048576 | tf_op jit(solution)/shard_map/all_to_all | solution.py:171
  37.0 3.8 %collective-permute-start = (bf16[8,16,640]{2,1,0:T(8,128)(2,1)S(1)}, bf16[8,16,640]{2,1,0:T(8,128)(2,1)S(1)}, u32[]{:S(2)}, u32[]{:S(2)}) collective-permute-start(bf16[8,16,640]{2,1,0:T(8,128)(2,1)S(1)} %all-to-all-done.own_ref), channel_id=1, source_target_pairs={{0,1},{1,0},{2,3},{3,2},{4,5},{5,4},{6,7},{7,6},{8,9},{9,8},{10,11... | collective-permute-start | bytes 491528 | tf_op jit(solution)/shard_map/ppermute | solution.py:167
  40.9 0.0 copy-done
  40.9 1.9 %collective-permute-start.1 = (bf16[128,512]{1,0:T(8,128)(2,1)S(1)}, bf16[128,512]{1,0:T(8,128)(2,1)S(1)}, u32[]{:S(2)}, u32[]{:S(2)}) collective-permute-start(bf16[128,512]{1,0:T(8,128)(2,1)S(1)} %convert_element_type.3.dir_ref), channel_id=1, source_target_pairs={{0,1},{1,0},{2,3},{3,2},{4,5},{5,4},{6,7},{7,6},{8,9},{9,8},{10,11... | collective-permute-start | bytes 393224 | tf_op jit(solution)/shard_map/ppermute | solution.py:167
  42.8 1.3 %collective-permute-done.1.mate_dir_ref = bf16[128,512]{1,0:T(8,128)(2,1)S(1)} collective-permute-done((bf16[128,512]{1,0:T(8,128)(2,1)S(1)}, bf16[128,512]{1,0:T(8,128)(2,1)S(1)}, u32[]{:S(2)}, u32[]{:S(2)}) %collective-permute-start.1) | collective-permute-done | bytes 131104 | tf_op jit(solution)/shard_map/ppermute | solution.py:167
  44.1 0.0 collective-permute-done.mate_ref
  44.1 6.9 %all-to-all-done.1.far_ref = bf16[32,64,128]{2,1,0:T(8,128)(2,1)S(1)} async-done(((bf16[32,64,128]{2,1,0:T(8,128)(2,1)}), bf16[32,64,128]{2,1,0:T(8,128)(2,1)S(1)}, u32[]{:S(2)}, u32[]{:S(2)}) %all-to-all-start.1) | async-done | bytes 524320 | tf_op jit(solution)/shard_map/all_to_all | solution.py:171
  51.1 13.0 %shard_map.96 = bf16[32,64,128]{2,1,0:T(8,128)(2,1)S(1)} custom-call(bf16[32,64,128]{2,1,0:T(8,128)(2,1)S(1)} %all-to-all-done.1.far_ref, bf16[8,16,640]{2,1,0:T(8,128)(2,1)S(1)} %all-to-all-done.own_ref, bf16[8,16,640]{2,1,0:T(8,128)(2,1)S(1)} %collective-permute-done.mate_ref, bf16[128,512]{1,0:T(8,128)(2,1)S(1)} %convert_element_type.3.dir_ref, ...), custom_call_target="tpu_custom_call" | custom-call | flops 9126805504 | bytes 2097152 | tf_op jit(solution)/shard_map/pallas_call | solution.py:38
  64.1 22.4 %all_to_all.25.parts_ref = bf16[32,64,128]{2,1,0:T(8,128)(2,1)S(1)} all-to-all(bf16[32,64,128]{2,1,0:T(8,128)(2,1)S(1)} %shard_map.96), channel_id=1, replica_groups=mesh['x'=4,'h'=2,'z'=8,'y'=4,'k'=2] {'z','y'}, dimensions={0} | all-to-all | bytes 1048576 | tf_op jit(solution)/shard_map/all_to_all | solution.py:171
  86.5 0.7 shard_map.97
  87.2 0.0 copy-start.1
  87.2 3.5 %all-to-all-start.3 = ((bf16[8,64,128]{2,1,0:T(8,128)(2,1)}), bf16[8,64,128]{2,1,0:T(8,128)(2,1)S(1)}, u32[]{:S(2)}, u32[]{:S(2)}) async-start(bf16[8,64,128]{2,1,0:T(8,128)(2,1)} %shard_map.97), calls=%async_computation.3 | async-start | bytes 262144 | tf_op jit(solution)/shard_map/all_to_all | solution.py:171
  91.4 8.7 %all-to-all-done.3.parts_ref = bf16[8,64,128]{2,1,0:T(8,128)(2,1)S(1)} async-done(((bf16[8,64,128]{2,1,0:T(8,128)(2,1)}), bf16[8,64,128]{2,1,0:T(8,128)(2,1)S(1)}, u32[]{:S(2)}, u32[]{:S(2)}) %all-to-all-start.3) | async-done | bytes 131104 | tf_op jit(solution)/shard_map/all_to_all | solution.py:171
  100.1 0.0 copy-done.1
  100.1 0.3 shard_map.98
  100.4 0.0 copy-start.2
  100.4 20.3 %all_to_all.26.sums_ref = f32[64,4,128]{2,1,0:T(4,128)S(1)} all-to-all(f32[64,4,128]{2,1,0:T(4,128)S(1)} %get-tuple-element.5), channel_id=1, replica_groups=mesh['x'=4,'h'=2,'z'=8,'y'=4,'k'=2] {'z','y','k'}, dimensions={0} | all-to-all | bytes 262144 | tf_op jit(solution)/shard_map/all_to_all | solution.py:171
  120.7 0.0 copy-done.2
  120.7 1.2 shard_map.99
  (1 shorter events, 0.0 us)
Async XLA Ops:
  0.6 0.7 copy-start.4
  1.3 0.8 copy-start.3
  3.4 19.8 %all-to-all-start = ((bf16[8,16,640]{2,1,0:T(8,128)(2,1)}), bf16[8,16,640]{2,1,0:T(8,128)(2,1)S(1)}, u32[]{:S(2)}, u32[]{:S(2)}) async-start(bf16[8,16,640]{2,1,0:T(8,128)(2,1)} %shard_map.94), calls=%async_computation | async-start | bytes 327680 | tf_op jit(solution)/shard_map/all_to_all | solution.py:171
  24.2 16.7 %copy-start = (f32[128,512]{1,0:T(8,128)S(1)}, f32[128,512]{1,0:T(8,128)}, u32[]{:S(2)}) copy-start(f32[128,512]{1,0:T(8,128)} %direction_ref.3) | copy-start | bytes 786436
  24.2 26.9 %all-to-all-start.1 = ((bf16[32,64,128]{2,1,0:T(8,128)(2,1)}), bf16[32,64,128]{2,1,0:T(8,128)(2,1)S(1)}, u32[]{:S(2)}, u32[]{:S(2)}) async-start(bf16[32,64,128]{2,1,0:T(8,128)(2,1)} %shard_map.95), calls=%async_computation.1 | async-start | bytes 1048576 | tf_op jit(solution)/shard_map/all_to_all | solution.py:171
  37.0 7.1 %collective-permute-start = (bf16[8,16,640]{2,1,0:T(8,128)(2,1)S(1)}, bf16[8,16,640]{2,1,0:T(8,128)(2,1)S(1)}, u32[]{:S(2)}, u32[]{:S(2)}) collective-permute-start(bf16[8,16,640]{2,1,0:T(8,128)(2,1)S(1)} %all-to-all-done.own_ref), channel_id=1, source_target_pairs={{0,1},{1,0},{2,3},{3,2},{4,5},{5,4},{6,7},{7,6},{8,9},{9,8},{10,11... | collective-permute-start | bytes 491528 | tf_op jit(solution)/shard_map/ppermute | solution.py:167
  40.9 3.2 %collective-permute-start.1 = (bf16[128,512]{1,0:T(8,128)(2,1)S(1)}, bf16[128,512]{1,0:T(8,128)(2,1)S(1)}, u32[]{:S(2)}, u32[]{:S(2)}) collective-permute-start(bf16[128,512]{1,0:T(8,128)(2,1)S(1)} %convert_element_type.3.dir_ref), channel_id=1, source_target_pairs={{0,1},{1,0},{2,3},{3,2},{4,5},{5,4},{6,7},{7,6},{8,9},{9,8},{10,11... | collective-permute-start | bytes 393224 | tf_op jit(solution)/shard_map/ppermute | solution.py:167
  87.2 12.9 %copy-start.1 = (f32[128,512]{1,0:T(8,128)S(1)}, f32[128,512]{1,0:T(8,128)}, u32[]{:S(2)}) copy-start(f32[128,512]{1,0:T(8,128)} %residual_ref.3) | copy-start | bytes 786436
  87.2 12.9 %all-to-all-start.3 = ((bf16[8,64,128]{2,1,0:T(8,128)(2,1)}), bf16[8,64,128]{2,1,0:T(8,128)(2,1)S(1)}, u32[]{:S(2)}, u32[]{:S(2)}) async-start(bf16[8,64,128]{2,1,0:T(8,128)(2,1)} %shard_map.97), calls=%async_computation.3 | async-start | bytes 262144 | tf_op jit(solution)/shard_map/all_to_all | solution.py:171
  100.4 20.3 %copy-start.2 = (f32[128,512]{1,0:T(8,128)S(1)}, f32[128,512]{1,0:T(8,128)}, u32[]{:S(2)}) copy-start(f32[128,512]{1,0:T(8,128)} %solution_ref.1) | copy-start | bytes 786436

commit v3 on v2

v3 whole, which is shorter than its diff:
```python
import jax
import jax.numpy as jnp
from jax import lax
from jax.experimental import pallas as pl
from jax.experimental.pallas import tpu as pltpu
from jax.sharding import Mesh, PartitionSpec as P

COMPS = 8
FEAT = 16
PROBES = 128
OWN = 512
SUB = OWN // COMPS
HALF = SUB // 2
BLOCK = 512
NAMES = ("x", "h", "u", "e", "y", "k")
SIZES = (4, 2, 4, 2, 4, 2)
COMP = ("x", "h")
PAIR = ("x", "h", "e")
CHIPS = ("u", "e", "y")
ROW = ("u", "e", "y", "k")
PLANE = 32
PARITY = tuple(tuple(i for i in range(PLANE) if i // 4 % 2 == e) for e in range(2))
ROWS = 64

bf16 = jnp.bfloat16
f32 = jnp.float32
VMEM = pl.BlockSpec(memory_space=pltpu.VMEM)
SMEM = pl.BlockSpec(memory_space=pltpu.SMEM)


def split3(value):
    first = value.astype(bf16)
    rest = value - first.astype(f32)
    second = rest.astype(bf16)
    rest = rest - second.astype(f32)
    return first, second, rest.astype(bf16)


def dot(a, b):
    return jnp.dot(a, b, preferred_element_type=f32)


def call(kernel, outs, in_specs, args, scratch=(), cost=None):
    return pl.pallas_call(
        kernel,
        out_shape=tuple(jax.ShapeDtypeStruct(shape, dtype) for shape, dtype in outs),
        in_specs=in_specs,
        out_specs=(VMEM,) * len(outs),
        scratch_shapes=scratch,
        compiler_params=pltpu.CompilerParams(vmem_limit_bytes=40 << 20),
        cost_estimate=cost,
    )(*args)


def scale_kernel(features_ref, length_ref, amplitude_ref, out_ref, features, length, amplitude, sems):
    copies = [
        pltpu.make_async_copy(features_ref, features, sems.at[0]),
        pltpu.make_async_copy(length_ref, length, sems.at[1]),
        pltpu.make_async_copy(amplitude_ref, amplitude, sems.at[2]),
    ]
    for copy in copies:
        copy.start()
    for copy in copies:
        copy.wait()
    eye = lax.broadcasted_iota(jnp.int32, (FEAT, FEAT), 0) == lax.broadcasted_iota(jnp.int32, (FEAT, FEAT), 1)
    wide = jnp.sum(jnp.where(eye, length[...], 0.0), axis=1, keepdims=True)
    scaled = (features[0] / wide).astype(bf16)
    a0, a1, a2 = (term.astype(f32) for term in split3(jnp.log(jnp.full((FEAT, 128), amplitude[0], f32))))
    row = lax.broadcasted_iota(jnp.int32, (FEAT, 128), 0)
    extra = jnp.where(row == 0, a0, jnp.where(row == 1, a1, jnp.where(row == 2, a2, 0.0))).astype(bf16)
    for index in range(2 * COMPS):
        out_ref[index, :, :OWN] = scaled
        out_ref[index, :, OWN:] = extra


def passing_kernel(place_ref, own_ref, out_ref, turned):
    columns = pl.ds(pl.multiple_of(place_ref[0] * 128, 128), 128)
    turned[...] = jnp.concatenate([own_ref[2 * c + place_ref[2], :, columns] for c in range(COMPS)]).T
    for side in range(2):
        piece = turned[pl.ds(pl.multiple_of(place_ref[1] * SUB + side * HALF, HALF), HALF), :]
        for index in PARITY[side]:
            out_ref[index] = piece


def weights_kernel(place_ref, far_ref, own_ref, mate_ref, dir_ref, mate_dir_ref, out_ref, lhs, dirs, rhs):
    parity = place_ref[2]
    for side in range(4):
        ref, side_dirs, odd = (own_ref, mate_ref)[side // 2], (dir_ref, mate_dir_ref)[side // 2], side % 2
        columns = slice(side * OWN, (side + 1) * OWN)
        dirs[columns, :] = side_dirs[parity if odd == 0 else 1 - parity].T
        for group in range(2):
            feats = jnp.concatenate([ref[2 * c + odd, :, :OWN] for c in range(4 * group, 4 * group + 4)])
            rhs[group, group * 64 : group * 64 + 64, columns] = feats
            offsets = []
            for c in range(4 * group, 4 * group + 4):
                near = ref[2 * c + odd].astype(f32)
                mine = near[:, :OWN]
                log_amp = jnp.sum(near[:, OWN:], axis=0, keepdims=True)[:, :1]
                offsets.append(log_amp - 0.5 * jnp.sum(mine * mine, axis=0, keepdims=True))
            terms = [term.astype(f32) for term in split3(jnp.concatenate(offsets))]
            tail = jnp.concatenate([jnp.ones((12, OWN), f32)] + terms + [jnp.zeros((40, OWN), f32)])
            rhs[group, 64 - group * 64 : 128 - group * 64, columns] = tail.astype(bf16)

    lane = lax.broadcasted_iota(jnp.int32, (256, 128), 1)
    spot = lane % 64
    upper = lane >= 64
    comp = lax.broadcasted_iota(jnp.int32, (128, 128), 0) // FEAT
    column = lax.broadcasted_iota(jnp.int32, (128, 128), 1)
    place = (comp % 4 == column % 4) & (column % 64 < 12) & ((comp < 4) == (column >= 64))
    place = jnp.where(place, -0.5, 0.0).astype(bf16)
    place = jnp.concatenate((place, place))
    for index in range(PLANE // 8):
        feats = far_ref[index * 8 : (index + 1) * 8].reshape(256, 128)
        wide = feats.astype(f32)
        square = wide * wide
        high = square.astype(bf16)
        low = (square - high.astype(f32)).astype(bf16)
        half = dot(jnp.concatenate((high, low), axis=1), place)
        a0, a1, a2 = (term.astype(f32) for term in split3(half))
        aux = jnp.where(spot < 8, jnp.where(spot < 4, a0, a1), jnp.where(spot < 12, a2, jnp.where(spot < 24, 1.0, 0.0)))
        rows = slice(index * 256, (index + 1) * 256)
        for c in range(COMPS):
            in_feats = upper if c >= 4 else jnp.logical_not(upper)
            keep = jnp.where(in_feats, spot // FEAT, spot % 4) == c % 4
            lhs[c, rows] = jnp.where(keep, jnp.where(in_feats, wide, aux), 0.0).astype(bf16)

    total = None
    for begin in range(0, 4 * OWN, BLOCK):
        columns = slice(begin, begin + BLOCK)
        weight = None
        for c in range(COMPS):
            term = jnp.exp(dot(lhs[c], rhs[c // 4, :, columns]))
            weight = term if weight is None else weight + term
        part = dot(weight.astype(bf16), dirs[columns, :])
        total = part if total is None else total + part
    out_ref[...] = total.astype(bf16).reshape(PLANE, HALF, PROBES)


def add_kernel(parts_ref, out_ref):
    for side in range(2):
        total = parts_ref[PARITY[side][0]].astype(f32)
        for index in PARITY[side][1:]:
            total = total + parts_ref[index].astype(f32)
        total = total.astype(bf16)
        for c in range(COMPS):
            out_ref[c, side * HALF : (side + 1) * HALF] = total


def image_kernel(noise_ref, parts_ref, direction_ref, residual_ref, image_ref, sums_ref):
    direction = direction_ref[...]
    residual = residual_ref[...]
    image = parts_ref[...].reshape(OWN, PROBES).astype(f32).T + noise_ref[0] * direction
    image_ref[...] = image
    terms = (residual * residual, direction * image, residual * image, image * image)
    lane = lax.broadcasted_iota(jnp.int32, (PROBES, 8), 1)
    sums = jnp.zeros((PROBES, 8), f32)
    for index, term in enumerate(terms):
        sums = jnp.where(lane == index, jnp.sum(term, axis=1, keepdims=True), sums)
    sums = sums.T[:4]
    for index in range(ROWS):
        sums_ref[index] = sums


def update_kernel(sums_ref, image_ref, solution_ref, residual_ref, direction_ref, outs_ref, outr_ref, outd_ref):
    sums = sums_ref[0]
    for index in range(1, ROWS):
        sums = sums + sums_ref[index]
    norm_now, curve, mixed, image_norm = (sums[index : index + 1] for index in range(4))
    alpha = norm_now / curve
    fresh = jnp.maximum(norm_now + alpha * (alpha * image_norm - 2.0 * mixed), 0.0)
    beta = fresh / norm_now
    line = lax.broadcasted_iota(jnp.int32, (8, PROBES), 0)
    scalars = jnp.where(line == 0, alpha, jnp.where(line == 1, beta, 0.0)).T
    alpha, beta = scalars[:, :1], scalars[:, 1:2]
    direction = direction_ref[...]
    outs_ref[...] = solution_ref[...] + alpha * direction
    new_residual = residual_ref[...] - alpha * image_ref[...]
    outr_ref[...] = new_residual
    outd_ref[...] = new_residual + beta * direction


def swap(value):
    return lax.ppermute(value, "k", ((0, 1), (1, 0)))


def exchange(value, axes):
    return lax.all_to_all(value, axes, 0, 0, tiled=True)


def local(features, lengthscale, amplitude, noise, solution, residual, direction):
    low = direction.astype(bf16)
    lows = jnp.stack((low, lax.ppermute(low, "e", ((0, 1), (1, 0)))))
    mate_lows = swap(lows)
    (own,) = call(
        scale_kernel,
        (((2 * COMPS, FEAT, OWN + 128), bf16),),
        (pl.BlockSpec(memory_space=pltpu.HBM),) * 3,
        (features, lengthscale, amplitude),
        (
            pltpu.VMEM((1, FEAT, OWN), f32),
            pltpu.VMEM((1, FEAT), f32),
            pltpu.SMEM((1,), f32),
            pltpu.SemaphoreType.DMA((3,)),
        ),
    )
    own = exchange(own, PAIR)
    mate = swap(own)

    place = jnp.stack([lax.axis_index(name) for name in ("x", "h", "e")]).astype(jnp.int32)
    far_shape = ((PLANE, HALF, PROBES), bf16)
    (far,) = call(passing_kernel, (far_shape,), (SMEM, VMEM), (place, own), (pltpu.VMEM((128, COMPS * FEAT), bf16),))
    far = exchange(far, CHIPS)
    points = PLANE * HALF
    (part,) = call(
        weights_kernel,
        (far_shape,),
        (SMEM,) + (VMEM,) * 5,
        (place, far, own, mate, lows, mate_lows),
        (
            pltpu.VMEM((COMPS, points, 128), bf16),
            pltpu.VMEM((4 * OWN, PROBES), bf16),
            pltpu.VMEM((2, 128, 4 * OWN), bf16),
        ),
        pl.CostEstimate(
            flops=8 * points * OWN * (COMPS * 256 + 128), bytes_accessed=2 << 20, transcendentals=4 * points * OWN * COMPS
        ),
    )
    (part,) = call(add_kernel, (((COMPS, SUB, PROBES), bf16),), (VMEM,), (exchange(part, CHIPS),))
    image, sums = call(
        image_kernel,
        (((PROBES, OWN), f32), ((ROWS, 4, PROBES), f32)),
        (SMEM, VMEM, VMEM, VMEM),
        (noise, exchange(part, COMP), direction, residual),
    )
    sums = exchange(sums, ROW)

    block = pl.BlockSpec((PROBES, OWN), lambda: (0, 0))
    return pl.pallas_call(
        update_kernel,
        out_shape=(jax.ShapeDtypeStruct((PROBES, OWN), f32),) * 3,
        in_specs=(VMEM,) * 5,
        out_specs=(block,) * 3,
        compiler_params=pltpu.CompilerParams(vmem_limit_bytes=40 << 20),
    )(sums, image, solution, residual, direction)


def solution(mesh):
    fine = Mesh(mesh.devices.reshape(SIZES), NAMES)
    comp, row = COMP, ROW
    in_specs = (
        P(comp, None, row),
        P(comp, None),
        P(comp),
        P(),
        P(None, row),
        P(None, row),
        P(None, row),
    )
    out_specs = (P(None, row), P(None, row), P(None, row))
    return jax.shard_map(local, mesh=fine, in_specs=in_specs, out_specs=out_specs, check_vma=False)
```

time: 122 us -> 116 us (0.951)
  blocking collectives: 42.7 us -> 35.5 us
  starting transfers between devices: 32.2 us -> 38.4 us
  waiting for transfers between devices: 26.7 us -> 21.7 us
    all_to_all x2, blocking collectives: 42.7 us -> 35.5 us  [exchange(): return lax.all_to_all(value, axes, 0, 0, tiled=True)]
    all_to_all x3, waiting for transfers between devices: 25.3 us -> 20.2 us  [exchange(): return lax.all_to_all(value, axes, 0, 0, tiled=True)]
    ppermute x0 -> x1, starting transfers between devices: none -> 3.27 us  [local(): lows = jnp.stack((low, lax.ppermute(low, 'e', ((0, 1), (1, 0)))))]
    all_to_all x3, starting transfers between devices: 26.5 us -> 29.5 us  [exchange(): return lax.all_to_all(value, axes, 0, 0, tiled=True)]
  transfers between devices with their start and end apart: 5 -> 6, of which waited for: 4 -> 4; matrix products, arithmetic and copies ran while one was open for 0% -> 0% of each run, Pallas kernels for 0% -> 1%
where the time goes in v3:
time: 116 us
  starting transfers between devices  38.4 us (33%)
  blocking collectives  35.5 us (31%)
  waiting for transfers between devices  21.7 us (19%)
  Pallas kernels  17.3 us (15%)
  between operations  2.1 us (2%)
    all_to_all x2, blocking collectives, exchange(): return lax.all_to_all(value, axes, 0, 0, tiled=True)  35.5 us
    all_to_all x3, starting transfers between devices, exchange(): return lax.all_to_all(value, axes, 0, 0, tiled=True)  29.5 us
    all_to_all x3, waiting for transfers between devices, exchange(): return lax.all_to_all(value, axes, 0, 0, tiled=True)  20.2 us
    pallas_call x5, Pallas kernels, call(): pl.pallas_call(kernel, out_shape=tuple((jax.ShapeDtypeStruct(shape, dtype...  16.1 us
    ppermute x2, starting transfers between devices, swap(): return lax.ppermute(value, 'k', ((0, 1), (1, 0)))  5.61 us
    ppermute x1, starting transfers between devices, local(): lows = jnp.stack((low, lax.ppermute(low, 'e', ((0, 1), (1, 0)))))  3.27 us
  transfers between devices with their start and end apart: 6, of which 4 were waited for; matrix products, arithmetic and copies ran while one was open for 0% of the time, Pallas kernels for 1%

profile of v3, /device:TPU:1, one launch (start us, length us, event | category | flops | bytes accessed | tf_op | source)
XLA Modules:
  0.0 115.9 jit_solution(3787265995298245271)
XLA Ops:
  0.6 0.0 copy-start.4
  1.3 0.0 copy-done.4
  1.3 0.0 copy-start.3
  1.3 0.7 copy-done.3
  2.1 1.4 %shard_map.94 = bf16[16,16,640]{2,1,0:T(8,128)(2,1)} custom-call(f32[1,16,512]{2,1,0:T(8,128)S(1)} %copy-done.3, f32[1,16]{1,0:T(1,128)S(1)} %copy-done.4, f32[1]{0:T(128)S(6)} %copy.10.amplitude_ref), custom_call_target="tpu_custom_call" | custom-call | tf_op jit(solution)/shard_map/pallas_call | solution.py:44
  3.5 0.0 copy-start
  3.5 12.2 %all-to-all-start = ((bf16[16,16,640]{2,1,0:T(8,128)(2,1)}), bf16[16,16,640]{2,1,0:T(8,128)(2,1)S(1)}, u32[]{:S(2)}, u32[]{:S(2)}) async-start(bf16[16,16,640]{2,1,0:T(8,128)(2,1)} %shard_map.94), calls=%async_computation | async-start | bytes 655360 | tf_op jit(solution)/shard_map/all_to_all | solution.py:187
  15.7 0.0 copy-done
  15.7 3.3 %collective-permute-start.1 = (bf16[128,512]{1,0:T(8,128)(2,1)S(1)}, bf16[128,512]{1,0:T(8,128)(2,1)S(1)}, u32[]{:S(2)}, u32[]{:S(2)}) collective-permute-start(bf16[128,512]{1,0:T(8,128)(2,1)S(1)} %convert_element_type.3), channel_id=1, source_target_pairs={{0,8},{8,0},{1,9},{9,1},{2,10},{10,2},{3,11},{11,3},{4,12},{12,4},... | collective-permute-start | bytes 393224 | tf_op jit(solution)/shard_map/ppermute | solution.py:192
  19.0 0.1 pad_add_fusion.place_ref
  19.1 7.8 %all-to-all-done.own_ref = bf16[16,16,640]{2,1,0:T(8,128)(2,1)S(1)} async-done(((bf16[16,16,640]{2,1,0:T(8,128)(2,1)}), bf16[16,16,640]{2,1,0:T(8,128)(2,1)S(1)}, u32[]{:S(2)}, u32[]{:S(2)}) %all-to-all-start) | async-done | bytes 327712 | tf_op jit(solution)/shard_map/all_to_all | solution.py:187
  26.9 1.4 %shard_map.95 = bf16[32,32,128]{2,1,0:T(8,128)(2,1)} custom-call(s32[3]{0:T(128)S(1)} %pad_add_fusion.place_ref, bf16[16,16,640]{2,1,0:T(8,128)(2,1)S(1)} %all-to-all-done.own_ref), custom_call_target="tpu_custom_call" | custom-call | tf_op jit(solution)/shard_map/pallas_call | solution.py:44
  28.2 14.0 %all-to-all-start.1 = ((bf16[32,32,128]{2,1,0:T(8,128)(2,1)}), bf16[32,32,128]{2,1,0:T(8,128)(2,1)S(1)}, u32[]{:S(2)}, u32[]{:S(2)}) async-start(bf16[32,32,128]{2,1,0:T(8,128)(2,1)} %shard_map.95), calls=%async_computation.1 | async-start | bytes 524288 | tf_op jit(solution)/shard_map/all_to_all | solution.py:187
  42.2 3.7 %collective-permute-start = (bf16[16,16,640]{2,1,0:T(8,128)(2,1)S(1)}, bf16[16,16,640]{2,1,0:T(8,128)(2,1)S(1)}, u32[]{:S(2)}, u32[]{:S(2)}) collective-permute-start(bf16[16,16,640]{2,1,0:T(8,128)(2,1)S(1)} %all-to-all-done.own_ref), channel_id=1, source_target_pairs={{0,1},{1,0},{2,3},{3,2},{4,5},{5,4},{6,7},{7,6},{8,9},{9,8},{10,11... | collective-permute-start | bytes 983048 | tf_op jit(solution)/shard_map/ppermute | solution.py:183
  45.9 0.0 collective-permute-done.1
  46.0 1.9 %collective-permute-start.2 = (bf16[2,128,512]{2,1,0:T(8,128)(2,1)S(1)}, bf16[2,128,512]{2,1,0:T(8,128)(2,1)S(1)}, u32[]{:S(2)}, u32[]{:S(2)}) collective-permute-start(bf16[2,128,512]{2,1,0:T(8,128)(2,1)S(1)} %pad_maximum_fusion.dir_ref), channel_id=1, source_target_pairs={{0,1},{1,0},{2,3},{3,2},{4,5},{5,4},{6,7},{7,6},{8,9},{9,8},{10,11... | collective-permute-start | bytes 786440 | tf_op jit(solution)/shard_map/ppermute | solution.py:183
  47.9 1.5 %collective-permute-done.2.mate_dir_ref = bf16[2,128,512]{2,1,0:T(8,128)(2,1)S(1)} collective-permute-done((bf16[2,128,512]{2,1,0:T(8,128)(2,1)S(1)}, bf16[2,128,512]{2,1,0:T(8,128)(2,1)S(1)}, u32[]{:S(2)}, u32[]{:S(2)}) %collective-permute-start.2) | collective-permute-done | bytes 262176 | tf_op jit(solution)/shard_map/ppermute | solution.py:183
  49.4 0.0 collective-permute-done.mate_ref
  49.4 3.7 %all-to-all-done.1.far_ref = bf16[32,32,128]{2,1,0:T(8,128)(2,1)S(1)} async-done(((bf16[32,32,128]{2,1,0:T(8,128)(2,1)}), bf16[32,32,128]{2,1,0:T(8,128)(2,1)S(1)}, u32[]{:S(2)}, u32[]{:S(2)}) %all-to-all-start.1) | async-done | bytes 262176 | tf_op jit(solution)/shard_map/all_to_all | solution.py:187
  53.1 12.4 %shard_map.96 = bf16[32,32,128]{2,1,0:T(8,128)(2,1)S(1)} custom-call(s32[3]{0:T(128)S(1)} %pad_add_fusion.place_ref, bf16[32,32,128]{2,1,0:T(8,128)(2,1)S(1)} %all-to-all-done.1.far_ref, bf16[16,16,640]{2,1,0:T(8,128)(2,1)S(1)} %all-to-all-done.own_ref, bf16[16,16,640]{2,1,0:T(8,128)(2,1)S(1)} %collective-permute-done.mate_ref, ...), custom_call_target="tpu_custom_call" | custom-call | flops 9126805504 | bytes 2097152 | tf_op jit(solution)/shard_map/pallas_call | solution.py:44
  65.5 17.7 %all_to_all.25.parts_ref = bf16[32,32,128]{2,1,0:T(8,128)(2,1)S(1)} all-to-all(bf16[32,32,128]{2,1,0:T(8,128)(2,1)S(1)} %shard_map.96), channel_id=1, replica_groups=mesh['x'=4,'h'=2,'u'=4,'e'=2,'y'=4,'k'=2] {'u','e','y'}, dimensions={0} | all-to-all | bytes 524288 | tf_op jit(solution)/shard_map/all_to_all | solution.py:187
  83.1 0.0 copy-start.1
  83.1 0.7 shard_map.97
  83.8 3.4 %all-to-all-start.3 = ((bf16[8,64,128]{2,1,0:T(8,128)(2,1)}), bf16[8,64,128]{2,1,0:T(8,128)(2,1)S(1)}, u32[]{:S(2)}, u32[]{:S(2)}) async-start(bf16[8,64,128]{2,1,0:T(8,128)(2,1)} %shard_map.97), calls=%async_computation.3 | async-start | bytes 262144 | tf_op jit(solution)/shard_map/all_to_all | solution.py:187
  87.9 8.7 %all-to-all-done.3.parts_ref = bf16[8,64,128]{2,1,0:T(8,128)(2,1)S(1)} async-done(((bf16[8,64,128]{2,1,0:T(8,128)(2,1)}), bf16[8,64,128]{2,1,0:T(8,128)(2,1)S(1)}, u32[]{:S(2)}, u32[]{:S(2)}) %all-to-all-start.3) | async-done | bytes 131104 | tf_op jit(solution)/shard_map/all_to_all | solution.py:187
  96.6 0.0 copy-done.1
  96.6 0.3 shard_map.98
  96.9 0.0 copy-start.2
  96.9 17.8 %all_to_all.26.sums_ref = f32[64,4,128]{2,1,0:T(4,128)S(1)} all-to-all(f32[64,4,128]{2,1,0:T(4,128)S(1)} %get-tuple-element.5), channel_id=1, replica_groups=mesh['x'=4,'h'=2,'u'=4,'e'=2,'y'=4,'k'=2] {'u','e','y','k'}, dimensions={0} | all-to-all | bytes 262144 | tf_op jit(solution)/shard_map/all_to_all | solution.py:187
  114.7 0.0 copy-done.2
  114.7 1.2 %shard_map.99 = (f32[128,512]{1,0:T(8,128)}, f32[128,512]{1,0:T(8,128)}, f32[128,512]{1,0:T(8,128)}) custom-call(f32[64,4,128]{2,1,0:T(4,128)S(1)} %all_to_all.26.sums_ref, f32[128,512]{1,0:T(8,128)S(1)} %get-tuple-element.6.image_ref, f32[128,512]{1,0:T(8,128)S(1)} %copy-done.2, f32[128,512]{1,0:T(8,128)S(1)} %copy-done.1, f32[128,512]{1,0:T(8,128)S(1)} %copy-done), custom_call_target="tpu_custom_call" | custom-call | tf_op jit(solution)/shard_map/pallas_call | solution.py:238
  (3 shorter events, 0.1 us)
Async XLA Ops:
  0.6 0.7 copy-start.4
  1.3 0.8 copy-start.3
  3.5 12.2 %copy-start = (f32[128,512]{1,0:T(8,128)S(1)}, f32[128,512]{1,0:T(8,128)}, u32[]{:S(2)}) copy-start(f32[128,512]{1,0:T(8,128)} %direction_ref.3) | copy-start | bytes 786436
  3.5 23.4 %all-to-all-start = ((bf16[16,16,640]{2,1,0:T(8,128)(2,1)}), bf16[16,16,640]{2,1,0:T(8,128)(2,1)S(1)}, u32[]{:S(2)}, u32[]{:S(2)}) async-start(bf16[16,16,640]{2,1,0:T(8,128)(2,1)} %shard_map.94), calls=%async_computation | async-start | bytes 655360 | tf_op jit(solution)/shard_map/all_to_all | solution.py:187
  15.7 30.2 %collective-permute-start.1 = (bf16[128,512]{1,0:T(8,128)(2,1)S(1)}, bf16[128,512]{1,0:T(8,128)(2,1)S(1)}, u32[]{:S(2)}, u32[]{:S(2)}) collective-permute-start(bf16[128,512]{1,0:T(8,128)(2,1)S(1)} %convert_element_type.3), channel_id=1, source_target_pairs={{0,8},{8,0},{1,9},{9,1},{2,10},{10,2},{3,11},{11,3},{4,12},{12,4},... | collective-permute-start | bytes 393224 | tf_op jit(solution)/shard_map/ppermute | solution.py:192
  28.2 24.9 %all-to-all-start.1 = ((bf16[32,32,128]{2,1,0:T(8,128)(2,1)}), bf16[32,32,128]{2,1,0:T(8,128)(2,1)S(1)}, u32[]{:S(2)}, u32[]{:S(2)}) async-start(bf16[32,32,128]{2,1,0:T(8,128)(2,1)} %shard_map.95), calls=%async_computation.1 | async-start | bytes 524288 | tf_op jit(solution)/shard_map/all_to_all | solution.py:187
  42.2 7.2 %collective-permute-start = (bf16[16,16,640]{2,1,0:T(8,128)(2,1)S(1)}, bf16[16,16,640]{2,1,0:T(8,128)(2,1)S(1)}, u32[]{:S(2)}, u32[]{:S(2)}) collective-permute-start(bf16[16,16,640]{2,1,0:T(8,128)(2,1)S(1)} %all-to-all-done.own_ref), channel_id=1, source_target_pairs={{0,1},{1,0},{2,3},{3,2},{4,5},{5,4},{6,7},{7,6},{8,9},{9,8},{10,11... | collective-permute-start | bytes 983048 | tf_op jit(solution)/shard_map/ppermute | solution.py:183
  46.0 3.4 %collective-permute-start.2 = (bf16[2,128,512]{2,1,0:T(8,128)(2,1)S(1)}, bf16[2,128,512]{2,1,0:T(8,128)(2,1)S(1)}, u32[]{:S(2)}, u32[]{:S(2)}) collective-permute-start(bf16[2,128,512]{2,1,0:T(8,128)(2,1)S(1)} %pad_maximum_fusion.dir_ref), channel_id=1, source_target_pairs={{0,1},{1,0},{2,3},{3,2},{4,5},{5,4},{6,7},{7,6},{8,9},{9,8},{10,11... | collective-permute-start | bytes 786440 | tf_op jit(solution)/shard_map/ppermute | solution.py:183
  83.1 13.5 %copy-start.1 = (f32[128,512]{1,0:T(8,128)S(1)}, f32[128,512]{1,0:T(8,128)}, u32[]{:S(2)}) copy-start(f32[128,512]{1,0:T(8,128)} %residual_ref.3) | copy-start | bytes 786436
  83.8 12.8 %all-to-all-start.3 = ((bf16[8,64,128]{2,1,0:T(8,128)(2,1)}), bf16[8,64,128]{2,1,0:T(8,128)(2,1)S(1)}, u32[]{:S(2)}, u32[]{:S(2)}) async-start(bf16[8,64,128]{2,1,0:T(8,128)(2,1)} %shard_map.97), calls=%async_computation.3 | async-start | bytes 262144 | tf_op jit(solution)/shard_map/all_to_all | solution.py:187
  96.9 17.8 %copy-start.2 = (f32[128,512]{1,0:T(8,128)S(1)}, f32[128,512]{1,0:T(8,128)}, u32[]{:S(2)}) copy-start(f32[128,512]{1,0:T(8,128)} %solution_ref.1) | copy-start | bytes 786436

commit v4 on v3

v4 whole, which is shorter than its diff:
```python
import jax
import jax.numpy as jnp
from jax import lax
from jax.experimental import pallas as pl
from jax.experimental.pallas import tpu as pltpu
from jax.sharding import Mesh, PartitionSpec as P

COMPS = 8
FEAT = 16
PROBES = 128
OWN = 512
MINE = 4
SUB = OWN // MINE
HALF = SUB // 2
BLOCK = 1024
ROW_BLOCK = 1024
NAMES = ("x", "h", "u", "e", "y", "k")
SIZES = (4, 2, 4, 2, 4, 2)
COMP = ("x", "h")
PAIR = ("x", "e")
CHIPS = ("u", "e", "y")
ROW = ("u", "e", "y", "k")
PLANE = 32
PARITY = tuple(tuple(i for i in range(PLANE) if i // 4 % 2 == e) for e in range(2))
ROWS = 64

bf16 = jnp.bfloat16
f32 = jnp.float32
VMEM = pl.BlockSpec(memory_space=pltpu.VMEM)
SMEM = pl.BlockSpec(memory_space=pltpu.SMEM)


def split3(value):
    first = value.astype(bf16)
    rest = value - first.astype(f32)
    second = rest.astype(bf16)
    rest = rest - second.astype(f32)
    return first, second, rest.astype(bf16)


def dot(a, b):
    return jnp.dot(a, b, preferred_element_type=f32)


def call(kernel, outs, in_specs, args, scratch=(), cost=None):
    return pl.pallas_call(
        kernel,
        out_shape=tuple(jax.ShapeDtypeStruct(shape, dtype) for shape, dtype in outs),
        in_specs=in_specs,
        out_specs=(VMEM,) * len(outs),
        scratch_shapes=scratch,
        compiler_params=pltpu.CompilerParams(vmem_limit_bytes=24 << 20),
        cost_estimate=cost,
    )(*args)


def scale_kernel(features_ref, length_ref, amplitude_ref, out_ref, features, length, amplitude, sems):
    copies = [
        pltpu.make_async_copy(features_ref, features, sems.at[0]),
        pltpu.make_async_copy(length_ref, length, sems.at[1]),
        pltpu.make_async_copy(amplitude_ref, amplitude, sems.at[2]),
    ]
    for copy in copies:
        copy.start()
    for copy in copies:
        copy.wait()
    eye = lax.broadcasted_iota(jnp.int32, (FEAT, FEAT), 0) == lax.broadcasted_iota(jnp.int32, (FEAT, FEAT), 1)
    wide = jnp.sum(jnp.where(eye, length[...], 0.0), axis=1, keepdims=True)
    scaled = (features[0] / wide).astype(bf16)
    a0, a1, a2 = (term.astype(f32) for term in split3(jnp.log(jnp.full((FEAT, 128), amplitude[0], f32))))
    row = lax.broadcasted_iota(jnp.int32, (FEAT, 128), 0)
    extra = jnp.where(row == 0, a0, jnp.where(row == 1, a1, jnp.where(row == 2, a2, 0.0))).astype(bf16)
    for index in range(2 * MINE):
        out_ref[index, :, :OWN] = scaled
        out_ref[index, :, OWN:] = extra


def passing_kernel(place_ref, own_ref, out_ref):
    columns = pl.ds(pl.multiple_of(place_ref[0] * SUB, SUB), SUB)
    feats = jnp.concatenate([own_ref[2 * c + place_ref[1], :, columns] for c in range(MINE)]).astype(f32)
    turned = jnp.concatenate((feats, pltpu.roll(feats, SUB - HALF // 2, 1))).T.astype(bf16)
    for side in range(2):
        piece = turned[side * HALF : side * HALF + HALF // 2]
        for index in PARITY[side]:
            out_ref[index] = piece


def near_kernel(place_ref, own_ref, mate_ref, dir_ref, mate_dir_ref, lhs_ref, dirs_ref):
    parity = place_ref[1]
    for side in range(4):
        ref, side_dirs, odd = (own_ref, mate_ref)[side // 2], (dir_ref, mate_dir_ref)[side // 2], side % 2
        points = slice(side * OWN, (side + 1) * OWN)
        dirs_ref[:, points] = side_dirs[parity if odd == 0 else 1 - parity]
        near = [ref[2 * c + odd].astype(f32) for c in range(MINE)]
        offsets = []
        for part in near:
            mine = part[:, :OWN]
            log_amp = jnp.sum(part[:, OWN:], axis=0, keepdims=True)[:, :1]
            offsets.append(log_amp - 0.5 * jnp.sum(mine * mine, axis=0, keepdims=True))
        terms = [term.astype(f32) for term in split3(jnp.concatenate(offsets))]
        rows = [part[:, :OWN] for part in near] + [jnp.ones((12, OWN), f32)] + terms + [jnp.zeros((40, OWN), f32)]
        lhs_ref[points, :] = jnp.concatenate(rows).T.astype(bf16)


def weights_kernel(far_ref, lhs, dirs, out_ref, rhs):
    line = lax.broadcasted_iota(jnp.int32, (64, 256), 0)
    for index in range(PLANE // 4):
        turned = far_ref[index * 4 : (index + 1) * 4].reshape(128, 128).astype(f32).T
        wide = jnp.concatenate((turned[:64], turned[64:]), axis=1)
        square = wide * wide
        half = [-0.5 * jnp.sum(square[c * FEAT : (c + 1) * FEAT], axis=0, keepdims=True) for c in range(MINE)]
        terms = [term.astype(f32) for term in split3(jnp.concatenate(half))]
        tail = jnp.concatenate(terms + [jnp.ones((12, 256), f32), jnp.zeros((40, 256), f32)])
        columns = slice(index * 256, (index + 1) * 256)
        for c in range(MINE):
            rhs[c, :64, columns] = jnp.where(line // FEAT == c, wide, 0.0).astype(bf16)
            rhs[c, 64:, columns] = jnp.where(line % 4 == c, tail, 0.0).astype(bf16)

    for begin in range(0, PLANE * HALF, BLOCK):
        columns = slice(begin, begin + BLOCK)
        total = None
        for top in range(0, 4 * OWN, ROW_BLOCK):
            rows = slice(top, top + ROW_BLOCK)
            weight = None
            for c in range(MINE):
                term = jnp.exp(dot(lhs[rows, :], rhs[c, :, columns]))
                weight = term if weight is None else weight + term
            part = dot(dirs[:, rows], weight.astype(bf16))
            total = part if total is None else total + part
        for index in range(begin // 256, (begin + BLOCK) // 256):
            shift = index * 256 - begin
            for side in range(2):
                piece = total[:, shift + side * 128 : shift + side * 128 + 128].T.astype(bf16).reshape(4, HALF // 2, PROBES)
                out_ref[index * 4 : (index + 1) * 4, side * (HALF // 2) : (side + 1) * (HALF // 2)] = piece


def add_kernel(parts_ref, out_ref):
    for side in range(2):
        total = parts_ref[PARITY[side][0]].astype(f32)
        for index in PARITY[side][1:]:
            total = total + parts_ref[index].astype(f32)
        total = total.astype(bf16)
        for c in range(COMPS):
            out_ref[c, side * HALF : (side + 1) * HALF] = total


def image_kernel(noise_ref, parts_ref, direction_ref, residual_ref, image_ref, sums_ref):
    direction = direction_ref[...]
    residual = residual_ref[...]
    parts = [parts_ref[2 * x].astype(f32) + parts_ref[2 * x + 1].astype(f32) for x in range(MINE)]
    image = jnp.concatenate(parts).T + noise_ref[0] * direction
    image_ref[...] = image
    terms = (residual * residual, direction * image, residual * image, image * image)
    lane = lax.broadcasted_iota(jnp.int32, (PROBES, 8), 1)
    sums = jnp.zeros((PROBES, 8), f32)
    for index, term in enumerate(terms):
        sums = jnp.where(lane == index, jnp.sum(term, axis=1, keepdims=True), sums)
    sums = sums.T[:4]
    for index in range(ROWS):
        sums_ref[index] = sums


def update_kernel(sums_ref, image_ref, solution_ref, residual_ref, direction_ref, outs_ref, outr_ref, outd_ref):
    sums = sums_ref[0]
    for index in range(1, ROWS):
        sums = sums + sums_ref[index]
    norm_now, curve, mixed, image_norm = (sums[index : index + 1] for index in range(4))
    alpha = norm_now / curve
    fresh = jnp.maximum(norm_now + alpha * (alpha * image_norm - 2.0 * mixed), 0.0)
    beta = fresh / norm_now
    line = lax.broadcasted_iota(jnp.int32, (8, PROBES), 0)
    scalars = jnp.where(line == 0, alpha, jnp.where(line == 1, beta, 0.0)).T
    alpha, beta = scalars[:, :1], scalars[:, 1:2]
    direction = direction_ref[...]
    outs_ref[...] = solution_ref[...] + alpha * direction
    new_residual = residual_ref[...] - alpha * image_ref[...]
    outr_ref[...] = new_residual
    outd_ref[...] = new_residual + beta * direction


def swap(value):
    return lax.ppermute(value, "k", ((0, 1), (1, 0)))


def exchange(value, axes):
    return lax.all_to_all(value, axes, 0, 0, tiled=True)


def local(features, lengthscale, amplitude, noise, solution, residual, direction):
    low = direction.astype(bf16)
    lows = jnp.stack((low, lax.ppermute(low, "e", ((0, 1), (1, 0)))))
    mate_lows = swap(lows)
    (own,) = call(
        scale_kernel,
        (((2 * MINE, FEAT, OWN + 128), bf16),),
        (pl.BlockSpec(memory_space=pltpu.HBM),) * 3,
        (features, lengthscale, amplitude),
        (
            pltpu.VMEM((1, FEAT, OWN), f32),
            pltpu.VMEM((1, FEAT), f32),
            pltpu.SMEM((1,), f32),
            pltpu.SemaphoreType.DMA((3,)),
        ),
    )
    own = exchange(own, PAIR)
    mate = swap(own)

    place = jnp.stack([lax.axis_index(name) for name in ("x", "e")]).astype(jnp.int32)
    (far,) = call(passing_kernel, (((PLANE, HALF // 2, 128), bf16),), (SMEM, VMEM), (place, own))
    far = exchange(far, CHIPS)
    points = PLANE * HALF
    near, dirs = call(
        near_kernel,
        (((4 * OWN, 128), bf16), ((PROBES, 4 * OWN), bf16)),
        (SMEM,) + (VMEM,) * 4,
        (place, own, mate, lows, mate_lows),
        cost=pl.CostEstimate(flops=1 << 20, bytes_accessed=2 << 20, transcendentals=0),
    )
    (part,) = call(
        weights_kernel,
        (((PLANE, HALF, PROBES), bf16),),
        (VMEM,) * 3,
        (far, near, dirs),
        (pltpu.VMEM((MINE, 128, points), bf16),),
        pl.CostEstimate(
            flops=8 * points * OWN * (MINE * 256 + 128), bytes_accessed=2 << 20, transcendentals=4 * points * OWN * MINE
        ),
    )
    (part,) = call(add_kernel, (((COMPS, SUB, PROBES), bf16),), (VMEM,), (exchange(part, CHIPS),))
    image, sums = call(
        image_kernel,
        (((PROBES, OWN), f32), ((ROWS, 4, PROBES), f32)),
        (SMEM, VMEM, VMEM, VMEM),
        (noise, exchange(part, COMP), direction, residual),
    )
    sums = exchange(sums, ROW)

    block = pl.BlockSpec((PROBES, OWN), lambda: (0, 0))
    return pl.pallas_call(
        update_kernel,
        out_shape=(jax.ShapeDtypeStruct((PROBES, OWN), f32),) * 3,
        in_specs=(VMEM,) * 5,
        out_specs=(block,) * 3,
        compiler_params=pltpu.CompilerParams(vmem_limit_bytes=24 << 20),
    )(sums, image, solution, residual, direction)


def solution(mesh):
    fine = Mesh(mesh.devices.reshape(SIZES), NAMES)
    comp, row = COMP, ROW
    in_specs = (
        P(comp, None, row),
        P(comp, None),
        P(comp),
        P(),
        P(None, row),
        P(None, row),
        P(None, row),
    )
    out_specs = (P(None, row), P(None, row), P(None, row))
    return jax.shard_map(local, mesh=fine, in_specs=in_specs, out_specs=out_specs, check_vma=False)
```

time: 116 us -> 114 us (0.983)
  blocking collectives: 35.5 us -> 44.6 us
  waiting for transfers between devices: 21.7 us -> 15.3 us
  starting transfers between devices: 38.4 us -> 33.8 us
    all_to_all x2, blocking collectives: 35.5 us -> 44.6 us  [exchange(): return lax.all_to_all(value, axes, 0, 0, tiled=True)]
    all_to_all x3, waiting for transfers between devices: 20.2 us -> 13.9 us  [exchange(): return lax.all_to_all(value, axes, 0, 0, tiled=True)]
    all_to_all x3, starting transfers between devices: 29.5 us -> 24 us  [exchange(): return lax.all_to_all(value, axes, 0, 0, tiled=True)]
    pallas_call x5 -> x6, Pallas kernels: 16.1 us -> 15.1 us  [call(): pl.pallas_call(kernel, out_shape=tuple((jax.ShapeDtypeStruct(shape, dtype...]
  transfers between devices with their start and end apart: 6 -> 6, of which waited for: 4 -> 4; matrix products, arithmetic and copies ran while one was open for 0% -> 0% of each run, Pallas kernels for 1% -> 2%
where the time goes in v4:
time: 114 us; the launch traced here: 113 us
  blocking collectives  44.6 us (39%)
  starting transfers between devices  33.8 us (30%)
  Pallas kernels  16.3 us (14%)
  waiting for transfers between devices  15.3 us (13%)
  between operations  2.09 us (2%)
    all_to_all x2, blocking collectives, exchange(): return lax.all_to_all(value, axes, 0, 0, tiled=True)  44.6 us
    all_to_all x3, starting transfers between devices, exchange(): return lax.all_to_all(value, axes, 0, 0, tiled=True)  24 us
    pallas_call x6, Pallas kernels, call(): pl.pallas_call(kernel, out_shape=tuple((jax.ShapeDtypeStruct(shape, dtype...  15.1 us
    all_to_all x3, waiting for transfers between devices, exchange(): return lax.all_to_all(value, axes, 0, 0, tiled=True)  13.9 us
    ppermute x2, starting transfers between devices, swap(): return lax.ppermute(value, 'k', ((0, 1), (1, 0)))  6.45 us
    ppermute x1, starting transfers between devices, local(): lows = jnp.stack((low, lax.ppermute(low, 'e', ((0, 1), (1, 0)))))  3.36 us
  transfers between devices with their start and end apart: 6, of which 4 were waited for; matrix products, arithmetic and copies ran while one was open for 0% of the time, Pallas kernels for 2%

profile of v4, /device:TPU:1, one launch (start us, length us, event | category | flops | bytes accessed | tf_op | source)
XLA Modules:
  0.0 113.0 jit_solution(10431832636713751925)
XLA Ops:
  0.6 0.0 copy-start.4
  1.3 0.0 copy-done.4
  1.3 0.0 copy-start.3
  1.3 0.7 copy-done.3
  2.1 0.0 copy-start
  2.1 1.4 %shard_map.94 = bf16[8,16,640]{2,1,0:T(8,128)(2,1)} custom-call(f32[1,16,512]{2,1,0:T(8,128)S(1)} %copy-done.3, f32[1,16]{1,0:T(1,128)S(1)} %copy-done.4, f32[1]{0:T(128)S(6)} %copy.10.amplitude_ref), custom_call_target="tpu_custom_call" | custom-call | tf_op jit(solution)/shard_map/pallas_call | solution.py:46
  3.4 6.7 %all-to-all-start = ((bf16[8,16,640]{2,1,0:T(8,128)(2,1)}), bf16[8,16,640]{2,1,0:T(8,128)(2,1)S(1)}, u32[]{:S(2)}, u32[]{:S(2)}) async-start(bf16[8,16,640]{2,1,0:T(8,128)(2,1)} %shard_map.94), calls=%async_computation | async-start | bytes 327680 | tf_op jit(solution)/shard_map/all_to_all | solution.py:186
  10.1 0.0 copy-done
  10.1 3.4 %collective-permute-start.1 = (bf16[128,512]{1,0:T(8,128)(2,1)S(1)}, bf16[128,512]{1,0:T(8,128)(2,1)S(1)}, u32[]{:S(2)}, u32[]{:S(2)}) collective-permute-start(bf16[128,512]{1,0:T(8,128)(2,1)S(1)} %convert_element_type.3), channel_id=1, source_target_pairs={{0,8},{8,0},{1,9},{9,1},{2,10},{10,2},{3,11},{11,3},{4,12},{12,4},... | collective-permute-start | bytes 393224 | tf_op jit(solution)/shard_map/ppermute | solution.py:191
  13.5 0.1 pad_add_fusion.place_ref
  13.6 2.2 %all-to-all-done.own_ref = bf16[8,16,640]{2,1,0:T(8,128)(2,1)S(1)} async-done(((bf16[8,16,640]{2,1,0:T(8,128)(2,1)}), bf16[8,16,640]{2,1,0:T(8,128)(2,1)S(1)}, u32[]{:S(2)}, u32[]{:S(2)}) %all-to-all-start) | async-done | bytes 163872 | tf_op jit(solution)/shard_map/all_to_all | solution.py:186
  15.8 1.4 %shard_map.95 = bf16[32,32,128]{2,1,0:T(8,128)(2,1)} custom-call(s32[2]{0:T(128)S(1)} %pad_add_fusion.place_ref, bf16[8,16,640]{2,1,0:T(8,128)(2,1)S(1)} %all-to-all-done.own_ref), custom_call_target="tpu_custom_call" | custom-call | tf_op jit(solution)/shard_map/pallas_call | solution.py:46
  17.2 12.6 %all-to-all-start.1 = ((bf16[32,32,128]{2,1,0:T(8,128)(2,1)}), bf16[32,32,128]{2,1,0:T(8,128)(2,1)S(1)}, u32[]{:S(2)}, u32[]{:S(2)}) async-start(bf16[32,32,128]{2,1,0:T(8,128)(2,1)} %shard_map.95), calls=%async_computation.1 | async-start | bytes 524288 | tf_op jit(solution)/shard_map/all_to_all | solution.py:186
  29.8 0.0 collective-permute-done.1
  29.9 4.5 %collective-permute-start.2 = (bf16[2,128,512]{2,1,0:T(8,128)(2,1)S(1)}, bf16[2,128,512]{2,1,0:T(8,128)(2,1)S(1)}, u32[]{:S(2)}, u32[]{:S(2)}) collective-permute-start(bf16[2,128,512]{2,1,0:T(8,128)(2,1)S(1)} %pad_maximum_fusion.dir_ref), channel_id=1, source_target_pairs={{0,1},{1,0},{2,3},{3,2},{4,5},{5,4},{6,7},{7,6},{8,9},{9,8},{10,11... | collective-permute-start | bytes 786440 | tf_op jit(solution)/shard_map/ppermute | solution.py:182
  34.4 1.9 %collective-permute-start = (bf16[8,16,640]{2,1,0:T(8,128)(2,1)S(1)}, bf16[8,16,640]{2,1,0:T(8,128)(2,1)S(1)}, u32[]{:S(2)}, u32[]{:S(2)}) collective-permute-start(bf16[8,16,640]{2,1,0:T(8,128)(2,1)S(1)} %all-to-all-done.own_ref), channel_id=1, source_target_pairs={{0,1},{1,0},{2,3},{3,2},{4,5},{5,4},{6,7},{7,6},{8,9},{9,8},{10,11... | collective-permute-start | bytes 491528 | tf_op jit(solution)/shard_map/ppermute | solution.py:182
  36.3 0.0 collective-permute-done.2.mate_dir_ref
  36.3 1.4 %collective-permute-done.mate_ref = bf16[8,16,640]{2,1,0:T(8,128)(2,1)S(1)} collective-permute-done((bf16[8,16,640]{2,1,0:T(8,128)(2,1)S(1)}, bf16[8,16,640]{2,1,0:T(8,128)(2,1)S(1)}, u32[]{:S(2)}, u32[]{:S(2)}) %collective-permute-start) | collective-permute-done | bytes 163872 | tf_op jit(solution)/shard_map/ppermute | solution.py:182
  37.7 0.9 shard_map.96
  38.6 2.2 %all-to-all-done.1.far_ref = bf16[32,32,128]{2,1,0:T(8,128)(2,1)S(1)} async-done(((bf16[32,32,128]{2,1,0:T(8,128)(2,1)}), bf16[32,32,128]{2,1,0:T(8,128)(2,1)S(1)}, u32[]{:S(2)}, u32[]{:S(2)}) %all-to-all-start.1) | async-done | bytes 262176 | tf_op jit(solution)/shard_map/all_to_all | solution.py:186
  40.8 10.5 %shard_map.97 = bf16[32,64,128]{2,1,0:T(8,128)(2,1)S(1)} custom-call(bf16[32,32,128]{2,1,0:T(8,128)(2,1)S(1)} %all-to-all-done.1.far_ref, bf16[2048,128]{1,0:T(8,128)(2,1)S(1)} %get-tuple-element.7.lhs, bf16[128,2048]{1,0:T(8,128)(2,1)S(1)} %get-tuple-element.8.dirs), custom_call_target="tpu_custom_call" | custom-call | flops 9663676416 | bytes 2097152 | tf_op jit(solution)/shard_map/pallas_call | solution.py:46
  51.2 23.0 %all_to_all.25.parts_ref = bf16[32,64,128]{2,1,0:T(8,128)(2,1)S(1)} all-to-all(bf16[32,64,128]{2,1,0:T(8,128)(2,1)S(1)} %shard_map.97), channel_id=1, replica_groups=mesh['x'=4,'h'=2,'u'=4,'e'=2,'y'=4,'k'=2] {'u','e','y'}, dimensions={0} | all-to-all | bytes 1048576 | tf_op jit(solution)/shard_map/all_to_all | solution.py:186
  74.2 0.8 shard_map.98
  75.0 0.0 copy-start.1
  75.0 4.7 %all-to-all-start.3 = ((bf16[8,128,128]{2,1,0:T(8,128)(2,1)}), bf16[8,128,128]{2,1,0:T(8,128)(2,1)S(1)}, u32[]{:S(2)}, u32[]{:S(2)}) async-start(bf16[8,128,128]{2,1,0:T(8,128)(2,1)} %shard_map.98), calls=%async_computation.3 | async-start | bytes 524288 | tf_op jit(solution)/shard_map/all_to_all | solution.py:186
  80.4 9.5 %all-to-all-done.3.parts_ref = bf16[8,128,128]{2,1,0:T(8,128)(2,1)S(1)} async-done(((bf16[8,128,128]{2,1,0:T(8,128)(2,1)}), bf16[8,128,128]{2,1,0:T(8,128)(2,1)S(1)}, u32[]{:S(2)}, u32[]{:S(2)}) %all-to-all-start.3) | async-done | bytes 262176 | tf_op jit(solution)/shard_map/all_to_all | solution.py:186
  89.9 0.0 copy-done.1
  89.9 0.3 shard_map.99
  90.2 0.0 copy-start.2
  90.2 21.6 %all_to_all.26.sums_ref = f32[64,4,128]{2,1,0:T(4,128)S(1)} all-to-all(f32[64,4,128]{2,1,0:T(4,128)S(1)} %get-tuple-element.9), channel_id=1, replica_groups=mesh['x'=4,'h'=2,'u'=4,'e'=2,'y'=4,'k'=2] {'u','e','y','k'}, dimensions={0} | all-to-all | bytes 262144 | tf_op jit(solution)/shard_map/all_to_all | solution.py:186
  111.8 0.0 copy-done.2
  111.8 1.2 %shard_map.100 = (f32[128,512]{1,0:T(8,128)}, f32[128,512]{1,0:T(8,128)}, f32[128,512]{1,0:T(8,128)}) custom-call(f32[64,4,128]{2,1,0:T(4,128)S(1)} %all_to_all.26.sums_ref, f32[128,512]{1,0:T(8,128)S(1)} %get-tuple-element.10.image_ref, f32[128,512]{1,0:T(8,128)S(1)} %copy-done.2, f32[128,512]{1,0:T(8,128)S(1)} %copy-done.1, f32[128,512]{1,0:T(8,128)S(1)} %copy-done), custom_call_target="tpu_custom_call" | custom-call | tf_op jit(solution)/shard_map/pallas_call | solution.py:239
  (3 shorter events, 0.1 us)
Async XLA Ops:
  0.6 0.7 copy-start.4
  1.3 0.8 copy-start.3
  2.1 8.0 %copy-start = (f32[128,512]{1,0:T(8,128)S(1)}, f32[128,512]{1,0:T(8,128)}, u32[]{:S(2)}) copy-start(f32[128,512]{1,0:T(8,128)} %direction_ref.3) | copy-start | bytes 786436
  3.4 12.3 %all-to-all-start = ((bf16[8,16,640]{2,1,0:T(8,128)(2,1)}), bf16[8,16,640]{2,1,0:T(8,128)(2,1)S(1)}, u32[]{:S(2)}, u32[]{:S(2)}) async-start(bf16[8,16,640]{2,1,0:T(8,128)(2,1)} %shard_map.94), calls=%async_computation | async-start | bytes 327680 | tf_op jit(solution)/shard_map/all_to_all | solution.py:186
  10.1 19.7 %collective-permute-start.1 = (bf16[128,512]{1,0:T(8,128)(2,1)S(1)}, bf16[128,512]{1,0:T(8,128)(2,1)S(1)}, u32[]{:S(2)}, u32[]{:S(2)}) collective-permute-start(bf16[128,512]{1,0:T(8,128)(2,1)S(1)} %convert_element_type.3), channel_id=1, source_target_pairs={{0,8},{8,0},{1,9},{9,1},{2,10},{10,2},{3,11},{11,3},{4,12},{12,4},... | collective-permute-start | bytes 393224 | tf_op jit(solution)/shard_map/ppermute | solution.py:191
  17.2 23.6 %all-to-all-start.1 = ((bf16[32,32,128]{2,1,0:T(8,128)(2,1)}), bf16[32,32,128]{2,1,0:T(8,128)(2,1)S(1)}, u32[]{:S(2)}, u32[]{:S(2)}) async-start(bf16[32,32,128]{2,1,0:T(8,128)(2,1)} %shard_map.95), calls=%async_computation.1 | async-start | bytes 524288 | tf_op jit(solution)/shard_map/all_to_all | solution.py:186
  29.9 6.5 %collective-permute-start.2 = (bf16[2,128,512]{2,1,0:T(8,128)(2,1)S(1)}, bf16[2,128,512]{2,1,0:T(8,128)(2,1)S(1)}, u32[]{:S(2)}, u32[]{:S(2)}) collective-permute-start(bf16[2,128,512]{2,1,0:T(8,128)(2,1)S(1)} %pad_maximum_fusion.dir_ref), channel_id=1, source_target_pairs={{0,1},{1,0},{2,3},{3,2},{4,5},{5,4},{6,7},{7,6},{8,9},{9,8},{10,11... | collective-permute-start | bytes 786440 | tf_op jit(solution)/shard_map/ppermute | solution.py:182
  34.4 3.3 %collective-permute-start = (bf16[8,16,640]{2,1,0:T(8,128)(2,1)S(1)}, bf16[8,16,640]{2,1,0:T(8,128)(2,1)S(1)}, u32[]{:S(2)}, u32[]{:S(2)}) collective-permute-start(bf16[8,16,640]{2,1,0:T(8,128)(2,1)S(1)} %all-to-all-done.own_ref), channel_id=1, source_target_pairs={{0,1},{1,0},{2,3},{3,2},{4,5},{5,4},{6,7},{7,6},{8,9},{9,8},{10,11... | collective-permute-start | bytes 491528 | tf_op jit(solution)/shard_map/ppermute | solution.py:182
  75.0 14.9 %copy-start.1 = (f32[128,512]{1,0:T(8,128)S(1)}, f32[128,512]{1,0:T(8,128)}, u32[]{:S(2)}) copy-start(f32[128,512]{1,0:T(8,128)} %residual_ref.3) | copy-start | bytes 786436
  75.0 14.9 %all-to-all-start.3 = ((bf16[8,128,128]{2,1,0:T(8,128)(2,1)}), bf16[8,128,128]{2,1,0:T(8,128)(2,1)S(1)}, u32[]{:S(2)}, u32[]{:S(2)}) async-start(bf16[8,128,128]{2,1,0:T(8,128)(2,1)} %shard_map.98), calls=%async_computation.3 | async-start | bytes 524288 | tf_op jit(solution)/shard_map/all_to_all | solution.py:186
  90.2 21.6 %copy-start.2 = (f32[128,512]{1,0:T(8,128)S(1)}, f32[128,512]{1,0:T(8,128)}, u32[]{:S(2)}) copy-start(f32[128,512]{1,0:T(8,128)} %solution_ref.1) | copy-start | bytes 786436

commit v5 on v4

--- a/solution.py
+++ b/solution.py
@@ -11,17 +11,16 @@
 OWN = 512
 MINE = 4
 SUB = OWN // MINE
-HALF = SUB // 2
+LEAP = SUB // 2
 BLOCK = 1024
 ROW_BLOCK = 1024
-NAMES = ("x", "h", "u", "e", "y", "k")
-SIZES = (4, 2, 4, 2, 4, 2)
+NAMES = ("x", "h", "z", "w", "e", "k")
+SIZES = (4, 2, 8, 2, 2, 2)
 COMP = ("x", "h")
 PAIR = ("x", "e")
-CHIPS = ("u", "e", "y")
-ROW = ("u", "e", "y", "k")
-PLANE = 32
-PARITY = tuple(tuple(i for i in range(PLANE) if i // 4 % 2 == e) for e in range(2))
+CHIPS = ("z", "w")
+ROW = ("z", "w", "e", "k")
+FAR = 16
 ROWS = 64
 
 bf16 = jnp.bfloat16
@@ -42,14 +41,14 @@
     return jnp.dot(a, b, preferred_element_type=f32)
 
 
-def call(kernel, outs, in_specs, args, scratch=(), cost=None):
+def call(kernel, outs, in_specs, args, scratch=(), cost=None, vmem=24 << 20):
     return pl.pallas_call(
         kernel,
         out_shape=tuple(jax.ShapeDtypeStruct(shape, dtype) for shape, dtype in outs),
         in_specs=in_specs,
         out_specs=(VMEM,) * len(outs),
         scratch_shapes=scratch,
-        compiler_params=pltpu.CompilerParams(vmem_limit_bytes=24 << 20),
+        compiler_params=pltpu.CompilerParams(vmem_limit_bytes=vmem),
         cost_estimate=cost,
     )(*args)
 
@@ -75,18 +74,17 @@
         out_ref[index, :, OWN:] = extra
 
 
-def passing_kernel(place_ref, own_ref, out_ref):
-    columns = pl.ds(pl.multiple_of(place_ref[0] * SUB, SUB), SUB)
-    feats = jnp.concatenate([own_ref[2 * c + place_ref[1], :, columns] for c in range(MINE)]).astype(f32)
-    turned = jnp.concatenate((feats, pltpu.roll(feats, SUB - HALF // 2, 1))).T.astype(bf16)
-    for side in range(2):
-        piece = turned[side * HALF : side * HALF + HALF // 2]
-        for index in PARITY[side]:
-            out_ref[index] = piece
-
-
-def near_kernel(place_ref, own_ref, mate_ref, dir_ref, mate_dir_ref, lhs_ref, dirs_ref):
-    parity = place_ref[1]
+def passing_kernel(own_ref, out_ref):
+    parity = lax.axis_index("e")
+    columns = pl.ds(pl.multiple_of(lax.axis_index("x") * SUB, SUB), SUB)
+    feats = jnp.concatenate([own_ref[2 * c + parity, :, columns] for c in range(MINE)]).astype(f32)
+    turned = jnp.concatenate((feats, pltpu.roll(feats, LEAP, 1))).T.astype(bf16)
+    for index in range(FAR):
+        out_ref[index] = turned[:LEAP]
+
+
+def near_kernel(own_ref, mate_ref, dir_ref, mate_dir_ref, lhs_ref, dirs_ref):
+    parity = lax.axis_index("e")
     for side in range(4):
         ref, side_dirs, odd = (own_ref, mate_ref)[side // 2], (dir_ref, mate_dir_ref)[side // 2], side % 2
         points = slice(side * OWN, (side + 1) * OWN)
@@ -104,8 +102,8 @@
 
 def weights_kernel(far_ref, lhs, dirs, out_ref, rhs):
     line = lax.broadcasted_iota(jnp.int32, (64, 256), 0)
-    for index in range(PLANE // 4):
-        turned = far_ref[index * 4 : (index + 1) * 4].reshape(128, 128).astype(f32).T
+    for index in range(FAR // 2):
+        turned = far_ref[index * 2 : (index + 1) * 2].reshape(128, 128).astype(f32).T
         wide = jnp.concatenate((turned[:64], turned[64:]), axis=1)
         square = wide * wide
         half = [-0.5 * jnp.sum(square[c * FEAT : (c + 1) * FEAT], axis=0, keepdims=True) for c in range(MINE)]
@@ -116,7 +114,7 @@
             rhs[c, :64, columns] = jnp.where(line // FEAT == c, wide, 0.0).astype(bf16)
             rhs[c, 64:, columns] = jnp.where(line % 4 == c, tail, 0.0).astype(bf16)
 
-    for begin in range(0, PLANE * HALF, BLOCK):
+    for begin in range(0, FAR * SUB, BLOCK):
         columns = slice(begin, begin + BLOCK)
         total = None
         for top in range(0, 4 * OWN, ROW_BLOCK):
@@ -130,18 +128,17 @@
         for index in range(begin // 256, (begin + BLOCK) // 256):
             shift = index * 256 - begin
             for side in range(2):
-                piece = total[:, shift + side * 128 : shift + side * 128 + 128].T.astype(bf16).reshape(4, HALF // 2, PROBES)
-                out_ref[index * 4 : (index + 1) * 4, side * (HALF // 2) : (side + 1) * (HALF // 2)] = piece
+                piece = total[:, shift + side * 128 : shift + side * 128 + 128].T.astype(bf16).reshape(2, LEAP, PROBES)
+                out_ref[index * 2 : (index + 1) * 2, side * LEAP : (side + 1) * LEAP] = piece
 
 
 def add_kernel(parts_ref, out_ref):
-    for side in range(2):
-        total = parts_ref[PARITY[side][0]].astype(f32)
-        for index in PARITY[side][1:]:
-            total = total + parts_ref[index].astype(f32)
-        total = total.astype(bf16)
-        for c in range(COMPS):
-            out_ref[c, side * HALF : (side + 1) * HALF] = total
+    total = parts_ref[0].astype(f32)
+    for index in range(1, FAR):
+        total = total + parts_ref[index].astype(f32)
+    total = total.astype(bf16)
+    for c in range(COMPS):
+        out_ref[c] = total
 
 
 def image_kernel(noise_ref, parts_ref, direction_ref, residual_ref, image_ref, sums_ref):
@@ -201,24 +198,24 @@
             pltpu.SMEM((1,), f32),
             pltpu.SemaphoreType.DMA((3,)),
         ),
+        vmem=60 << 20,
     )
     own = exchange(own, PAIR)
     mate = swap(own)
 
-    place = jnp.stack([lax.axis_index(name) for name in ("x", "e")]).astype(jnp.int32)
-    (far,) = call(passing_kernel, (((PLANE, HALF // 2, 128), bf16),), (SMEM, VMEM), (place, own))
+    (far,) = call(passing_kernel, (((FAR, LEAP, 128), bf16),), (VMEM,), (own,))
     far = exchange(far, CHIPS)
-    points = PLANE * HALF
+    points = FAR * SUB
     near, dirs = call(
         near_kernel,
         (((4 * OWN, 128), bf16), ((PROBES, 4 * OWN), bf16)),
-        (SMEM,) + (VMEM,) * 4,
-        (place, own, mate, lows, mate_lows),
+        (VMEM,) * 4,
+        (own, mate, lows, mate_lows),
         cost=pl.CostEstimate(flops=1 << 20, bytes_accessed=2 << 20, transcendentals=0),
     )
     (part,) = call(
         weights_kernel,
-        (((PLANE, HALF, PROBES), bf16),),
+        (((FAR, SUB, PROBES), bf16),),
         (VMEM,) * 3,
         (far, near, dirs),
         (pltpu.VMEM((MINE, 128, points), bf16),),

time: 114 us -> 109 us (0.956)
  blocking collectives: 44.6 us -> 43.1 us
  starting transfers between devices: 33.8 us -> 32.3 us
    all_to_all x2, blocking collectives: 44.6 us -> 43.1 us  [exchange(): return lax.all_to_all(value, axes, 0, 0, tiled=True)]
    all_to_all x3, starting transfers between devices: 24 us -> 22.5 us  [exchange(): return lax.all_to_all(value, axes, 0, 0, tiled=True)]
  transfers between devices with their start and end apart: 6 -> 6, of which waited for: 4 -> 4; matrix products, arithmetic and copies ran while one was open for 0% -> 0% of each run, Pallas kernels for 2% -> 1%
where the time goes in v5:
time: 109 us; the launch traced here: 108 us
  blocking collectives  43.1 us (40%)
  starting transfers between devices  32.3 us (30%)
  waiting for transfers between devices  15.7 us (14%)
  Pallas kernels  15.2 us (14%)
  between operations  2.05 us (2%)
    all_to_all x2, blocking collectives, exchange(): return lax.all_to_all(value, axes, 0, 0, tiled=True)  43.1 us
    all_to_all x3, starting transfers between devices, exchange(): return lax.all_to_all(value, axes, 0, 0, tiled=True)  22.5 us
    all_to_all x3, waiting for transfers between devices, exchange(): return lax.all_to_all(value, axes, 0, 0, tiled=True)  14.3 us
    pallas_call x6, Pallas kernels, call(): pl.pallas_call(kernel, out_shape=tuple((jax.ShapeDtypeStruct(shape, dtype...  14.1 us
    ppermute x2, starting transfers between devices, swap(): return lax.ppermute(value, 'k', ((0, 1), (1, 0)))  6.45 us
    ppermute x1, starting transfers between devices, local(): lows = jnp.stack((low, lax.ppermute(low, 'e', ((0, 1), (1, 0)))))  3.36 us
  transfers between devices with their start and end apart: 6, of which 4 were waited for; matrix products, arithmetic and copies ran while one was open for 0% of the time, Pallas kernels for 1%

profile of v5, /device:TPU:1, one launch (start us, length us, event | category | flops | bytes accessed | tf_op | source)
XLA Modules:
  0.0 108.4 jit_solution(10044291884114089030)
XLA Ops:
  1.3 0.0 copy-start
  1.3 1.6 %shard_map.94 = bf16[8,16,640]{2,1,0:T(8,128)(2,1)} custom-call(f32[1,16,512]{2,1,0:T(8,128)} %features_ref.1, f32[1,16]{1,0:T(1,128)} %length_ref.1, f32[1]{0:T(128)S(6)} %copy.10.amplitude_ref), custom_call_target="tpu_custom_call" | custom-call | tf_op jit(solution)/shard_map/pallas_call | solution.py:45
  2.9 5.9 %all-to-all-start = ((bf16[8,16,640]{2,1,0:T(8,128)(2,1)}), bf16[8,16,640]{2,1,0:T(8,128)(2,1)S(1)}, u32[]{:S(2)}, u32[]{:S(2)}) async-start(bf16[8,16,640]{2,1,0:T(8,128)(2,1)} %shard_map.94), calls=%async_computation | async-start | bytes 327680 | tf_op jit(solution)/shard_map/all_to_all | solution.py:183
  8.8 0.0 copy-done
  8.8 3.4 %collective-permute-start.1 = (bf16[128,512]{1,0:T(8,128)(2,1)S(1)}, bf16[128,512]{1,0:T(8,128)(2,1)S(1)}, u32[]{:S(2)}, u32[]{:S(2)}) collective-permute-start(bf16[128,512]{1,0:T(8,128)(2,1)S(1)} %convert_element_type.3), channel_id=1, source_target_pairs={{0,2},{2,0},{1,3},{3,1},{4,6},{6,4},{5,7},{7,5},{8,10},{10,8},{9,1... | collective-permute-start | bytes 393224 | tf_op jit(solution)/shard_map/ppermute | solution.py:188
  12.2 2.3 %all-to-all-done.own_ref = bf16[8,16,640]{2,1,0:T(8,128)(2,1)S(1)} async-done(((bf16[8,16,640]{2,1,0:T(8,128)(2,1)}), bf16[8,16,640]{2,1,0:T(8,128)(2,1)S(1)}, u32[]{:S(2)}, u32[]{:S(2)}) %all-to-all-start) | async-done | bytes 163872 | tf_op jit(solution)/shard_map/all_to_all | solution.py:183
  14.4 0.9 shard_map.95
  15.3 12.2 %all-to-all-start.1 = ((bf16[16,64,128]{2,1,0:T(8,128)(2,1)}), bf16[16,64,128]{2,1,0:T(8,128)(2,1)S(1)}, u32[]{:S(2)}, u32[]{:S(2)}) async-start(bf16[16,64,128]{2,1,0:T(8,128)(2,1)} %shard_map.95), calls=%async_computation.1 | async-start | bytes 524288 | tf_op jit(solution)/shard_map/all_to_all | solution.py:183
  27.5 0.0 collective-permute-done.1
  27.6 4.5 %collective-permute-start.2 = (bf16[2,128,512]{2,1,0:T(8,128)(2,1)S(1)}, bf16[2,128,512]{2,1,0:T(8,128)(2,1)S(1)}, u32[]{:S(2)}, u32[]{:S(2)}) collective-permute-start(bf16[2,128,512]{2,1,0:T(8,128)(2,1)S(1)} %pad_maximum_fusion.dir_ref), channel_id=1, source_target_pairs={{0,1},{1,0},{2,3},{3,2},{4,5},{5,4},{6,7},{7,6},{8,9},{9,8},{10,11... | collective-permute-start | bytes 786440 | tf_op jit(solution)/shard_map/ppermute | solution.py:179
  32.1 1.9 %collective-permute-start = (bf16[8,16,640]{2,1,0:T(8,128)(2,1)S(1)}, bf16[8,16,640]{2,1,0:T(8,128)(2,1)S(1)}, u32[]{:S(2)}, u32[]{:S(2)}) collective-permute-start(bf16[8,16,640]{2,1,0:T(8,128)(2,1)S(1)} %all-to-all-done.own_ref), channel_id=1, source_target_pairs={{0,1},{1,0},{2,3},{3,2},{4,5},{5,4},{6,7},{7,6},{8,9},{9,8},{10,11... | collective-permute-start | bytes 491528 | tf_op jit(solution)/shard_map/ppermute | solution.py:179
  34.1 0.0 collective-permute-done.2.mate_dir_ref
  34.1 1.4 %collective-permute-done.mate_ref = bf16[8,16,640]{2,1,0:T(8,128)(2,1)S(1)} collective-permute-done((bf16[8,16,640]{2,1,0:T(8,128)(2,1)S(1)}, bf16[8,16,640]{2,1,0:T(8,128)(2,1)S(1)}, u32[]{:S(2)}, u32[]{:S(2)}) %collective-permute-start) | collective-permute-done | bytes 163872 | tf_op jit(solution)/shard_map/ppermute | solution.py:179
  35.4 0.3 shard_map.96
  35.8 2.5 %all-to-all-done.1.far_ref = bf16[16,64,128]{2,1,0:T(8,128)(2,1)S(1)} async-done(((bf16[16,64,128]{2,1,0:T(8,128)(2,1)}), bf16[16,64,128]{2,1,0:T(8,128)(2,1)S(1)}, u32[]{:S(2)}, u32[]{:S(2)}) %all-to-all-start.1) | async-done | bytes 262176 | tf_op jit(solution)/shard_map/all_to_all | solution.py:183
  38.3 10.2 %shard_map.97 = bf16[16,128,128]{2,1,0:T(8,128)(2,1)S(1)} custom-call(bf16[16,64,128]{2,1,0:T(8,128)(2,1)S(1)} %all-to-all-done.1.far_ref, bf16[2048,128]{1,0:T(8,128)(2,1)S(1)} %get-tuple-element.7.lhs, bf16[128,2048]{1,0:T(8,128)(2,1)S(1)} %get-tuple-element.8.dirs), custom_call_target="tpu_custom_call" | custom-call | flops 9663676416 | bytes 2097152 | tf_op jit(solution)/shard_map/pallas_call | solution.py:45
  48.5 25.6 %all_to_all.25.parts_ref = bf16[16,128,128]{2,1,0:T(8,128)(2,1)S(1)} all-to-all(bf16[16,128,128]{2,1,0:T(8,128)(2,1)S(1)} %shard_map.97), channel_id=1, replica_groups=mesh['x'=4,'h'=2,'z'=8,'w'=2,'e'=2,'k'=2] {'z','w'}, dimensions={0} | all-to-all | bytes 1048576 | tf_op jit(solution)/shard_map/all_to_all | solution.py:183
  74.1 0.8 shard_map.98
  74.9 0.0 copy-start.1
  74.9 4.4 %all-to-all-start.3 = ((bf16[8,128,128]{2,1,0:T(8,128)(2,1)}), bf16[8,128,128]{2,1,0:T(8,128)(2,1)S(1)}, u32[]{:S(2)}, u32[]{:S(2)}) async-start(bf16[8,128,128]{2,1,0:T(8,128)(2,1)} %shard_map.98), calls=%async_computation.3 | async-start | bytes 524288 | tf_op jit(solution)/shard_map/all_to_all | solution.py:183
  80.0 9.5 %all-to-all-done.3.parts_ref = bf16[8,128,128]{2,1,0:T(8,128)(2,1)S(1)} async-done(((bf16[8,128,128]{2,1,0:T(8,128)(2,1)}), bf16[8,128,128]{2,1,0:T(8,128)(2,1)S(1)}, u32[]{:S(2)}, u32[]{:S(2)}) %all-to-all-start.3) | async-done | bytes 262176 | tf_op jit(solution)/shard_map/all_to_all | solution.py:183
  89.5 0.0 copy-done.1
  89.5 0.3 shard_map.99
  89.8 0.0 copy-start.2
  89.8 17.5 %all_to_all.26.sums_ref = f32[64,4,128]{2,1,0:T(4,128)S(1)} all-to-all(f32[64,4,128]{2,1,0:T(4,128)S(1)} %get-tuple-element.9), channel_id=1, replica_groups=mesh['x'=4,'h'=2,'z'=8,'w'=2,'e'=2,'k'=2] {'z','w','e','k'}, dimensions={0} | all-to-all | bytes 262144 | tf_op jit(solution)/shard_map/all_to_all | solution.py:183
  107.3 0.0 copy-done.2
  107.3 1.2 %shard_map.100 = (f32[128,512]{1,0:T(8,128)}, f32[128,512]{1,0:T(8,128)}, f32[128,512]{1,0:T(8,128)}) custom-call(f32[64,4,128]{2,1,0:T(4,128)S(1)} %all_to_all.26.sums_ref, f32[128,512]{1,0:T(8,128)S(1)} %get-tuple-element.10.image_ref, f32[128,512]{1,0:T(8,128)S(1)} %copy-done.2, f32[128,512]{1,0:T(8,128)S(1)} %copy-done.1, f32[128,512]{1,0:T(8,128)S(1)} %copy-done), custom_call_target="tpu_custom_call" | custom-call | tf_op jit(solution)/shard_map/pallas_call | solution.py:236
  (3 shorter events, 0.1 us)
Async XLA Ops:
  1.3 7.5 %copy-start = (f32[128,512]{1,0:T(8,128)S(1)}, f32[128,512]{1,0:T(8,128)}, u32[]{:S(2)}) copy-start(f32[128,512]{1,0:T(8,128)} %direction_ref.3) | copy-start | bytes 786436
  2.9 11.6 %all-to-all-start = ((bf16[8,16,640]{2,1,0:T(8,128)(2,1)}), bf16[8,16,640]{2,1,0:T(8,128)(2,1)S(1)}, u32[]{:S(2)}, u32[]{:S(2)}) async-start(bf16[8,16,640]{2,1,0:T(8,128)(2,1)} %shard_map.94), calls=%async_computation | async-start | bytes 327680 | tf_op jit(solution)/shard_map/all_to_all | solution.py:183
  8.8 18.7 %collective-permute-start.1 = (bf16[128,512]{1,0:T(8,128)(2,1)S(1)}, bf16[128,512]{1,0:T(8,128)(2,1)S(1)}, u32[]{:S(2)}, u32[]{:S(2)}) collective-permute-start(bf16[128,512]{1,0:T(8,128)(2,1)S(1)} %convert_element_type.3), channel_id=1, source_target_pairs={{0,2},{2,0},{1,3},{3,1},{4,6},{6,4},{5,7},{7,5},{8,10},{10,8},{9,1... | collective-permute-start | bytes 393224 | tf_op jit(solution)/shard_map/ppermute | solution.py:188
  15.3 23.0 %all-to-all-start.1 = ((bf16[16,64,128]{2,1,0:T(8,128)(2,1)}), bf16[16,64,128]{2,1,0:T(8,128)(2,1)S(1)}, u32[]{:S(2)}, u32[]{:S(2)}) async-start(bf16[16,64,128]{2,1,0:T(8,128)(2,1)} %shard_map.95), calls=%async_computation.1 | async-start | bytes 524288 | tf_op jit(solution)/shard_map/all_to_all | solution.py:183
  27.6 6.5 %collective-permute-start.2 = (bf16[2,128,512]{2,1,0:T(8,128)(2,1)S(1)}, bf16[2,128,512]{2,1,0:T(8,128)(2,1)S(1)}, u32[]{:S(2)}, u32[]{:S(2)}) collective-permute-start(bf16[2,128,512]{2,1,0:T(8,128)(2,1)S(1)} %pad_maximum_fusion.dir_ref), channel_id=1, source_target_pairs={{0,1},{1,0},{2,3},{3,2},{4,5},{5,4},{6,7},{7,6},{8,9},{9,8},{10,11... | collective-permute-start | bytes 786440 | tf_op jit(solution)/shard_map/ppermute | solution.py:179
  32.1 3.3 %collective-permute-start = (bf16[8,16,640]{2,1,0:T(8,128)(2,1)S(1)}, bf16[8,16,640]{2,1,0:T(8,128)(2,1)S(1)}, u32[]{:S(2)}, u32[]{:S(2)}) collective-permute-start(bf16[8,16,640]{2,1,0:T(8,128)(2,1)S(1)} %all-to-all-done.own_ref), channel_id=1, source_target_pairs={{0,1},{1,0},{2,3},{3,2},{4,5},{5,4},{6,7},{7,6},{8,9},{9,8},{10,11... | collective-permute-start | bytes 491528 | tf_op jit(solution)/shard_map/ppermute | solution.py:179
  74.9 14.6 %copy-start.1 = (f32[128,512]{1,0:T(8,128)S(1)}, f32[128,512]{1,0:T(8,128)}, u32[]{:S(2)}) copy-start(f32[128,512]{1,0:T(8,128)} %residual_ref.3) | copy-start | bytes 786436
  74.9 14.6 %all-to-all-start.3 = ((bf16[8,128,128]{2,1,0:T(8,128)(2,1)}), bf16[8,128,128]{2,1,0:T(8,128)(2,1)S(1)}, u32[]{:S(2)}, u32[]{:S(2)}) async-start(bf16[8,128,128]{2,1,0:T(8,128)(2,1)} %shard_map.98), calls=%async_computation.3 | async-start | bytes 524288 | tf_op jit(solution)/shard_map/all_to_all | solution.py:183
  89.8 17.5 %copy-start.2 = (f32[128,512]{1,0:T(8,128)S(1)}, f32[128,512]{1,0:T(8,128)}, u32[]{:S(2)}) copy-start(f32[128,512]{1,0:T(8,128)} %solution_ref.1) | copy-start | bytes 786436

commit v6 on v5

--- a/solution.py
+++ b/solution.py
@@ -83,13 +83,13 @@
         out_ref[index] = turned[:LEAP]
 
 
-def near_kernel(own_ref, mate_ref, dir_ref, mate_dir_ref, lhs_ref, dirs_ref):
+def near_kernel(feats_ref, dir_ref, lhs_ref, dirs_ref):
     parity = lax.axis_index("e")
     for side in range(4):
-        ref, side_dirs, odd = (own_ref, mate_ref)[side // 2], (dir_ref, mate_dir_ref)[side // 2], side % 2
+        core, odd = side // 2, side % 2
         points = slice(side * OWN, (side + 1) * OWN)
-        dirs_ref[:, points] = side_dirs[parity if odd == 0 else 1 - parity]
-        near = [ref[2 * c + odd].astype(f32) for c in range(MINE)]
+        dirs_ref[:, points] = dir_ref[2 * core + (parity if odd == 0 else 1 - parity)]
+        near = [feats_ref[core, 2 * c + odd].astype(f32) for c in range(MINE)]
         offsets = []
         for part in near:
             mine = part[:, :OWN]
@@ -175,10 +175,6 @@
     outd_ref[...] = new_residual + beta * direction
 
 
-def swap(value):
-    return lax.ppermute(value, "k", ((0, 1), (1, 0)))
-
-
 def exchange(value, axes):
     return lax.all_to_all(value, axes, 0, 0, tiled=True)
 
@@ -186,7 +182,7 @@
 def local(features, lengthscale, amplitude, noise, solution, residual, direction):
     low = direction.astype(bf16)
     lows = jnp.stack((low, lax.ppermute(low, "e", ((0, 1), (1, 0)))))
-    mate_lows = swap(lows)
+    lows = lax.all_gather(lows, "k", axis=0, tiled=True)
     (own,) = call(
         scale_kernel,
         (((2 * MINE, FEAT, OWN + 128), bf16),),
@@ -201,7 +197,7 @@
         vmem=60 << 20,
     )
     own = exchange(own, PAIR)
-    mate = swap(own)
+    feats = lax.all_gather(own, "k")
 
     (far,) = call(passing_kernel, (((FAR, LEAP, 128), bf16),), (VMEM,), (own,))
     far = exchange(far, CHIPS)
@@ -209,8 +205,8 @@
     near, dirs = call(
         near_kernel,
         (((4 * OWN, 128), bf16), ((PROBES, 4 * OWN), bf16)),
-        (VMEM,) * 4,
-        (own, mate, lows, mate_lows),
+        (VMEM,) * 2,
+        (feats, lows),
         cost=pl.CostEstimate(flops=1 << 20, bytes_accessed=2 << 20, transcendentals=0),
     )
     (part,) = call(

time: 109 us -> 108 us (level)
  starting transfers between devices: 32.3 us -> 25.9 us
  blocking collectives: 43.1 us -> 48 us
    all_gather x0 -> x2, blocking collectives: none -> 6.47 us  [the longest x1 4.43 us: local(): lows = lax.all_gather(lows, 'k', axis=0, tiled=True)]
    ppermute x2 -> x0, starting transfers between devices: 6.45 us -> none  [swap(): return lax.ppermute(value, 'k', ((0, 1), (1, 0)))]
    all_to_all x2, blocking collectives: 43.1 us -> 41.6 us  [exchange(): return lax.all_to_all(value, axes, 0, 0, tiled=True)]
    all_to_all x3, waiting for transfers between devices: 14.3 us -> 15.7 us  [exchange(): return lax.all_to_all(value, axes, 0, 0, tiled=True)]
    ppermute x2 -> x0, waiting for transfers between devices: 1.35 us -> none  [swap(): return lax.ppermute(value, 'k', ((0, 1), (1, 0)))]
  transfers between devices with their start and end apart: 6 -> 4, of which waited for: 4 -> 3; matrix products, arithmetic and copies ran while one was open for 0% -> 0% of each run, Pallas kernels for 1% -> 1%
where the time goes in v6:
time: 108 us; the launch traced here: 107 us
  blocking collectives  48 us (44%)
  starting transfers between devices  25.9 us (24%)
  waiting for transfers between devices  15.7 us (15%)
  Pallas kernels  15.2 us (14%)
  between operations  2.03 us (2%)
    all_to_all x2, blocking collectives, exchange(): return lax.all_to_all(value, axes, 0, 0, tiled=True)  41.6 us
    all_to_all x3, starting transfers between devices, exchange(): return lax.all_to_all(value, axes, 0, 0, tiled=True)  22.6 us
    all_to_all x3, waiting for transfers between devices, exchange(): return lax.all_to_all(value, axes, 0, 0, tiled=True)  15.7 us
    pallas_call x6, Pallas kernels, call(): pl.pallas_call(kernel, out_shape=tuple((jax.ShapeDtypeStruct(shape, dtype...  14.1 us
    all_gather x1, blocking collectives, local(): lows = lax.all_gather(lows, 'k', axis=0, tiled=True)  4.43 us
    ppermute x1, starting transfers between devices, local(): lows = jnp.stack((low, lax.ppermute(low, 'e', ((0, 1), (1, 0)))))  3.36 us
  transfers between devices with their start and end apart: 4, of which 3 were waited for; matrix products, arithmetic and copies ran while one was open for 0% of the time, Pallas kernels for 1%

profile of v6, /device:TPU:1, one launch (start us, length us, event | category | flops | bytes accessed | tf_op | source)
XLA Modules:
  0.0 107.0 jit_solution(18363908948069593136)
XLA Ops:
  1.3 0.0 copy-start
  1.3 1.6 %shard_map.94 = bf16[8,16,640]{2,1,0:T(8,128)(2,1)} custom-call(f32[1,16,512]{2,1,0:T(8,128)} %features_ref.1, f32[1,16]{1,0:T(1,128)} %length_ref.1, f32[1]{0:T(128)S(6)} %copy.10.amplitude_ref), custom_call_target="tpu_custom_call" | custom-call | tf_op jit(solution)/shard_map/pallas_call | solution.py:45
  2.9 5.9 %all-to-all-start = ((bf16[8,16,640]{2,1,0:T(8,128)(2,1)}), bf16[8,16,640]{2,1,0:T(8,128)(2,1)S(1)}, u32[]{:S(2)}, u32[]{:S(2)}) async-start(bf16[8,16,640]{2,1,0:T(8,128)(2,1)} %shard_map.94), calls=%async_computation | async-start | bytes 327680 | tf_op jit(solution)/shard_map/all_to_all | solution.py:179
  8.8 0.0 copy-done
  8.8 3.4 %collective-permute-start = (bf16[128,512]{1,0:T(8,128)(2,1)S(1)}, bf16[128,512]{1,0:T(8,128)(2,1)S(1)}, u32[]{:S(2)}, u32[]{:S(2)}) collective-permute-start(bf16[128,512]{1,0:T(8,128)(2,1)S(1)} %convert_element_type.3), channel_id=1, source_target_pairs={{0,2},{2,0},{1,3},{3,1},{4,6},{6,4},{5,7},{7,5},{8,10},{10,8},{9,1... | collective-permute-start | bytes 393224 | tf_op jit(solution)/shard_map/ppermute | solution.py:184
  12.2 2.3 %all-to-all-done.own_ref = bf16[8,16,640]{2,1,0:T(8,128)(2,1)S(1)} async-done(((bf16[8,16,640]{2,1,0:T(8,128)(2,1)}), bf16[8,16,640]{2,1,0:T(8,128)(2,1)S(1)}, u32[]{:S(2)}, u32[]{:S(2)}) %all-to-all-start) | async-done | bytes 163872 | tf_op jit(solution)/shard_map/all_to_all | solution.py:179
  14.4 0.9 shard_map.95
  15.3 12.2 %all-to-all-start.1 = ((bf16[16,64,128]{2,1,0:T(8,128)(2,1)}), bf16[16,64,128]{2,1,0:T(8,128)(2,1)S(1)}, u32[]{:S(2)}, u32[]{:S(2)}) async-start(bf16[16,64,128]{2,1,0:T(8,128)(2,1)} %shard_map.95), calls=%async_computation.1 | async-start | bytes 524288 | tf_op jit(solution)/shard_map/all_to_all | solution.py:179
  27.5 0.0 collective-permute-done
  27.6 4.4 %all_gather.11.dir_ref = bf16[4,128,512]{2,1,0:T(8,128)(2,1)S(1)} all-gather(bf16[2,128,512]{2,1,0:T(8,128)(2,1)S(1)} %pad_maximum_fusion), channel_id=1, replica_groups=mesh['x'=4,'h'=2,'z'=8,'w'=2,'e'=2,'k'=2] {'k'}, dimensions={0}, use_global_device_ids=true | all-gather | bytes 786432 | tf_op jit(solution)/shard_map/all_gather | solution.py:185
  32.0 2.0 %all-gather = bf16[16,16,640]{2,1,0:T(8,128)(2,1)S(1)} all-gather(bf16[8,16,640]{2,1,0:T(8,128)(2,1)S(1)} %all-to-all-done.own_ref), channel_id=2, replica_groups=mesh['x'=4,'h'=2,'z'=8,'w'=2,'e'=2,'k'=2] {'k'}, dimensions={0}, use_global_device_ids=true | all-gather | bytes 491520 | tf_op jit(solution)/shard_map/all_gather | solution.py:200
  34.1 0.3 shard_map.96
  34.4 3.9 %all-to-all-done.1.far_ref = bf16[16,64,128]{2,1,0:T(8,128)(2,1)S(1)} async-done(((bf16[16,64,128]{2,1,0:T(8,128)(2,1)}), bf16[16,64,128]{2,1,0:T(8,128)(2,1)S(1)}, u32[]{:S(2)}, u32[]{:S(2)}) %all-to-all-start.1) | async-done | bytes 262176 | tf_op jit(solution)/shard_map/all_to_all | solution.py:179
  38.3 10.2 %shard_map.97 = bf16[16,128,128]{2,1,0:T(8,128)(2,1)S(1)} custom-call(bf16[16,64,128]{2,1,0:T(8,128)(2,1)S(1)} %all-to-all-done.1.far_ref, bf16[2048,128]{1,0:T(8,128)(2,1)S(1)} %get-tuple-element.7.lhs, bf16[128,2048]{1,0:T(8,128)(2,1)S(1)} %get-tuple-element.8.dirs), custom_call_target="tpu_custom_call" | custom-call | flops 9663676416 | bytes 2097152 | tf_op jit(solution)/shard_map/pallas_call | solution.py:45
  48.5 23.8 %all_to_all.25.parts_ref = bf16[16,128,128]{2,1,0:T(8,128)(2,1)S(1)} all-to-all(bf16[16,128,128]{2,1,0:T(8,128)(2,1)S(1)} %shard_map.97), channel_id=1, replica_groups=mesh['x'=4,'h'=2,'z'=8,'w'=2,'e'=2,'k'=2] {'z','w'}, dimensions={0} | all-to-all | bytes 1048576 | tf_op jit(solution)/shard_map/all_to_all | solution.py:179
  72.3 0.8 shard_map.98
  73.1 0.0 copy-start.1
  73.1 4.5 %all-to-all-start.3 = ((bf16[8,128,128]{2,1,0:T(8,128)(2,1)}), bf16[8,128,128]{2,1,0:T(8,128)(2,1)S(1)}, u32[]{:S(2)}, u32[]{:S(2)}) async-start(bf16[8,128,128]{2,1,0:T(8,128)(2,1)} %shard_map.98), calls=%async_computation.3 | async-start | bytes 524288 | tf_op jit(solution)/shard_map/all_to_all | solution.py:179
  78.2 9.5 %all-to-all-done.3.parts_ref = bf16[8,128,128]{2,1,0:T(8,128)(2,1)S(1)} async-done(((bf16[8,128,128]{2,1,0:T(8,128)(2,1)}), bf16[8,128,128]{2,1,0:T(8,128)(2,1)S(1)}, u32[]{:S(2)}, u32[]{:S(2)}) %all-to-all-start.3) | async-done | bytes 262176 | tf_op jit(solution)/shard_map/all_to_all | solution.py:179
  87.7 0.0 copy-done.1
  87.7 0.3 shard_map.99
  88.0 0.0 copy-start.2
  88.0 17.8 %all_to_all.26.sums_ref = f32[64,4,128]{2,1,0:T(4,128)S(1)} all-to-all(f32[64,4,128]{2,1,0:T(4,128)S(1)} %get-tuple-element.9), channel_id=1, replica_groups=mesh['x'=4,'h'=2,'z'=8,'w'=2,'e'=2,'k'=2] {'z','w','e','k'}, dimensions={0} | all-to-all | bytes 262144 | tf_op jit(solution)/shard_map/all_to_all | solution.py:179
  105.8 0.0 copy-done.2
  105.8 1.2 %shard_map.100 = (f32[128,512]{1,0:T(8,128)}, f32[128,512]{1,0:T(8,128)}, f32[128,512]{1,0:T(8,128)}) custom-call(f32[64,4,128]{2,1,0:T(4,128)S(1)} %all_to_all.26.sums_ref, f32[128,512]{1,0:T(8,128)S(1)} %get-tuple-element.10.image_ref, f32[128,512]{1,0:T(8,128)S(1)} %copy-done.2, f32[128,512]{1,0:T(8,128)S(1)} %copy-done.1, f32[128,512]{1,0:T(8,128)S(1)} %copy-done), custom_call_target="tpu_custom_call" | custom-call | tf_op jit(solution)/shard_map/pallas_call | solution.py:232
  (3 shorter events, 0.1 us)
Async XLA Ops:
  1.3 7.5 %copy-start = (f32[128,512]{1,0:T(8,128)S(1)}, f32[128,512]{1,0:T(8,128)}, u32[]{:S(2)}) copy-start(f32[128,512]{1,0:T(8,128)} %direction_ref.3) | copy-start | bytes 786436
  2.9 11.6 %all-to-all-start = ((bf16[8,16,640]{2,1,0:T(8,128)(2,1)}), bf16[8,16,640]{2,1,0:T(8,128)(2,1)S(1)}, u32[]{:S(2)}, u32[]{:S(2)}) async-start(bf16[8,16,640]{2,1,0:T(8,128)(2,1)} %shard_map.94), calls=%async_computation | async-start | bytes 327680 | tf_op jit(solution)/shard_map/all_to_all | solution.py:179
  8.8 18.7 %collective-permute-start = (bf16[128,512]{1,0:T(8,128)(2,1)S(1)}, bf16[128,512]{1,0:T(8,128)(2,1)S(1)}, u32[]{:S(2)}, u32[]{:S(2)}) collective-permute-start(bf16[128,512]{1,0:T(8,128)(2,1)S(1)} %convert_element_type.3), channel_id=1, source_target_pairs={{0,2},{2,0},{1,3},{3,1},{4,6},{6,4},{5,7},{7,5},{8,10},{10,8},{9,1... | collective-permute-start | bytes 393224 | tf_op jit(solution)/shard_map/ppermute | solution.py:184
  15.3 23.0 %all-to-all-start.1 = ((bf16[16,64,128]{2,1,0:T(8,128)(2,1)}), bf16[16,64,128]{2,1,0:T(8,128)(2,1)S(1)}, u32[]{:S(2)}, u32[]{:S(2)}) async-start(bf16[16,64,128]{2,1,0:T(8,128)(2,1)} %shard_map.95), calls=%async_computation.1 | async-start | bytes 524288 | tf_op jit(solution)/shard_map/all_to_all | solution.py:179
  73.1 14.6 %copy-start.1 = (f32[128,512]{1,0:T(8,128)S(1)}, f32[128,512]{1,0:T(8,128)}, u32[]{:S(2)}) copy-start(f32[128,512]{1,0:T(8,128)} %residual_ref.3) | copy-start | bytes 786436
  73.1 14.6 %all-to-all-start.3 = ((bf16[8,128,128]{2,1,0:T(8,128)(2,1)}), bf16[8,128,128]{2,1,0:T(8,128)(2,1)S(1)}, u32[]{:S(2)}, u32[]{:S(2)}) async-start(bf16[8,128,128]{2,1,0:T(8,128)(2,1)} %shard_map.98), calls=%async_computation.3 | async-start | bytes 524288 | tf_op jit(solution)/shard_map/all_to_all | solution.py:179
  88.0 17.8 %copy-start.2 = (f32[128,512]{1,0:T(8,128)S(1)}, f32[128,512]{1,0:T(8,128)}, u32[]{:S(2)}) copy-start(f32[128,512]{1,0:T(8,128)} %solution_ref.1) | copy-start | bytes 786436

commit v7 on v6

--- a/solution.py
+++ b/solution.py
@@ -13,7 +13,7 @@
 SUB = OWN // MINE
 LEAP = SUB // 2
 BLOCK = 1024
-ROW_BLOCK = 1024
+ROW_BLOCK = 2048
 NAMES = ("x", "h", "z", "w", "e", "k")
 SIZES = (4, 2, 8, 2, 2, 2)
 COMP = ("x", "h")

time: 108 us -> 108 us (level)
  no operation moved by 1% of the time
where the time goes in v7:
time: 108 us; the launch traced here: 107 us
  blocking collectives  48.1 us (45%)
  starting transfers between devices  25.9 us (24%)
  waiting for transfers between devices  15.7 us (15%)
  Pallas kernels  15.2 us (14%)
  between operations  2.03 us (2%)
    all_to_all x2, blocking collectives, exchange(): return lax.all_to_all(value, axes, 0, 0, tiled=True)  41.6 us
    all_to_all x3, starting transfers between devices, exchange(): return lax.all_to_all(value, axes, 0, 0, tiled=True)  22.5 us
    all_to_all x3, waiting for transfers between devices, exchange(): return lax.all_to_all(value, axes, 0, 0, tiled=True)  15.7 us
    pallas_call x6, Pallas kernels, call(): pl.pallas_call(kernel, out_shape=tuple((jax.ShapeDtypeStruct(shape, dtype...  14.1 us
    all_gather x1, blocking collectives, local(): lows = lax.all_gather(lows, 'k', axis=0, tiled=True)  4.43 us
    ppermute x1, starting transfers between devices, local(): lows = jnp.stack((low, lax.ppermute(low, 'e', ((0, 1), (1, 0)))))  3.36 us
  transfers between devices with their start and end apart: 4, of which 3 were waited for; matrix products, arithmetic and copies ran while one was open for 0% of the time, Pallas kernels for 1%

profile of v7, /device:TPU:1, one launch (start us, length us, event | category | flops | bytes accessed | tf_op | source)
XLA Modules:
  0.0 107.0 jit_solution(15583183476619113211)
XLA Ops:
  1.3 0.0 copy-start
  1.3 1.6 %shard_map.94 = bf16[8,16,640]{2,1,0:T(8,128)(2,1)} custom-call(f32[1,16,512]{2,1,0:T(8,128)} %features_ref.1, f32[1,16]{1,0:T(1,128)} %length_ref.1, f32[1]{0:T(128)S(6)} %copy.10.amplitude_ref), custom_call_target="tpu_custom_call" | custom-call | tf_op jit(solution)/shard_map/pallas_call | solution.py:45
  2.9 5.9 %all-to-all-start = ((bf16[8,16,640]{2,1,0:T(8,128)(2,1)}), bf16[8,16,640]{2,1,0:T(8,128)(2,1)S(1)}, u32[]{:S(2)}, u32[]{:S(2)}) async-start(bf16[8,16,640]{2,1,0:T(8,128)(2,1)} %shard_map.94), calls=%async_computation | async-start | bytes 327680 | tf_op jit(solution)/shard_map/all_to_all | solution.py:179
  8.8 0.0 copy-done
  8.8 3.4 %collective-permute-start = (bf16[128,512]{1,0:T(8,128)(2,1)S(1)}, bf16[128,512]{1,0:T(8,128)(2,1)S(1)}, u32[]{:S(2)}, u32[]{:S(2)}) collective-permute-start(bf16[128,512]{1,0:T(8,128)(2,1)S(1)} %convert_element_type.3), channel_id=1, source_target_pairs={{0,2},{2,0},{1,3},{3,1},{4,6},{6,4},{5,7},{7,5},{8,10},{10,8},{9,1... | collective-permute-start | bytes 393224 | tf_op jit(solution)/shard_map/ppermute | solution.py:184
  12.2 2.3 %all-to-all-done.own_ref = bf16[8,16,640]{2,1,0:T(8,128)(2,1)S(1)} async-done(((bf16[8,16,640]{2,1,0:T(8,128)(2,1)}), bf16[8,16,640]{2,1,0:T(8,128)(2,1)S(1)}, u32[]{:S(2)}, u32[]{:S(2)}) %all-to-all-start) | async-done | bytes 163872 | tf_op jit(solution)/shard_map/all_to_all | solution.py:179
  14.4 0.9 shard_map.95
  15.3 12.2 %all-to-all-start.1 = ((bf16[16,64,128]{2,1,0:T(8,128)(2,1)}), bf16[16,64,128]{2,1,0:T(8,128)(2,1)S(1)}, u32[]{:S(2)}, u32[]{:S(2)}) async-start(bf16[16,64,128]{2,1,0:T(8,128)(2,1)} %shard_map.95), calls=%async_computation.1 | async-start | bytes 524288 | tf_op jit(solution)/shard_map/all_to_all | solution.py:179
  27.5 0.0 collective-permute-done
  27.6 4.4 %all_gather.11.dir_ref = bf16[4,128,512]{2,1,0:T(8,128)(2,1)S(1)} all-gather(bf16[2,128,512]{2,1,0:T(8,128)(2,1)S(1)} %pad_maximum_fusion), channel_id=1, replica_groups=mesh['x'=4,'h'=2,'z'=8,'w'=2,'e'=2,'k'=2] {'k'}, dimensions={0}, use_global_device_ids=true | all-gather | bytes 786432 | tf_op jit(solution)/shard_map/all_gather | solution.py:185
  32.0 2.0 %all-gather = bf16[16,16,640]{2,1,0:T(8,128)(2,1)S(1)} all-gather(bf16[8,16,640]{2,1,0:T(8,128)(2,1)S(1)} %all-to-all-done.own_ref), channel_id=2, replica_groups=mesh['x'=4,'h'=2,'z'=8,'w'=2,'e'=2,'k'=2] {'k'}, dimensions={0}, use_global_device_ids=true | all-gather | bytes 491520 | tf_op jit(solution)/shard_map/all_gather | solution.py:200
  34.1 0.3 shard_map.96
  34.4 3.9 %all-to-all-done.1.far_ref = bf16[16,64,128]{2,1,0:T(8,128)(2,1)S(1)} async-done(((bf16[16,64,128]{2,1,0:T(8,128)(2,1)}), bf16[16,64,128]{2,1,0:T(8,128)(2,1)S(1)}, u32[]{:S(2)}, u32[]{:S(2)}) %all-to-all-start.1) | async-done | bytes 262176 | tf_op jit(solution)/shard_map/all_to_all | solution.py:179
  38.3 10.2 %shard_map.97 = bf16[16,128,128]{2,1,0:T(8,128)(2,1)S(1)} custom-call(bf16[16,64,128]{2,1,0:T(8,128)(2,1)S(1)} %all-to-all-done.1.far_ref, bf16[2048,128]{1,0:T(8,128)(2,1)S(1)} %get-tuple-element.7.lhs, bf16[128,2048]{1,0:T(8,128)(2,1)S(1)} %get-tuple-element.8.dirs), custom_call_target="tpu_custom_call" | custom-call | flops 9663676416 | bytes 2097152 | tf_op jit(solution)/shard_map/pallas_call | solution.py:45
  48.5 23.8 %all_to_all.25.parts_ref = bf16[16,128,128]{2,1,0:T(8,128)(2,1)S(1)} all-to-all(bf16[16,128,128]{2,1,0:T(8,128)(2,1)S(1)} %shard_map.97), channel_id=1, replica_groups=mesh['x'=4,'h'=2,'z'=8,'w'=2,'e'=2,'k'=2] {'z','w'}, dimensions={0} | all-to-all | bytes 1048576 | tf_op jit(solution)/shard_map/all_to_all | solution.py:179
  72.3 0.8 shard_map.98
  73.1 0.0 copy-start.1
  73.1 4.4 %all-to-all-start.3 = ((bf16[8,128,128]{2,1,0:T(8,128)(2,1)}), bf16[8,128,128]{2,1,0:T(8,128)(2,1)S(1)}, u32[]{:S(2)}, u32[]{:S(2)}) async-start(bf16[8,128,128]{2,1,0:T(8,128)(2,1)} %shard_map.98), calls=%async_computation.3 | async-start | bytes 524288 | tf_op jit(solution)/shard_map/all_to_all | solution.py:179
  78.2 9.5 %all-to-all-done.3.parts_ref = bf16[8,128,128]{2,1,0:T(8,128)(2,1)S(1)} async-done(((bf16[8,128,128]{2,1,0:T(8,128)(2,1)}), bf16[8,128,128]{2,1,0:T(8,128)(2,1)S(1)}, u32[]{:S(2)}, u32[]{:S(2)}) %all-to-all-start.3) | async-done | bytes 262176 | tf_op jit(solution)/shard_map/all_to_all | solution.py:179
  87.7 0.0 copy-done.1
  87.7 0.3 shard_map.99
  88.0 0.0 copy-start.2
  88.0 17.8 %all_to_all.26.sums_ref = f32[64,4,128]{2,1,0:T(4,128)S(1)} all-to-all(f32[64,4,128]{2,1,0:T(4,128)S(1)} %get-tuple-element.9), channel_id=1, replica_groups=mesh['x'=4,'h'=2,'z'=8,'w'=2,'e'=2,'k'=2] {'z','w','e','k'}, dimensions={0} | all-to-all | bytes 262144 | tf_op jit(solution)/shard_map/all_to_all | solution.py:179
  105.8 0.0 copy-done.2
  105.8 1.2 %shard_map.100 = (f32[128,512]{1,0:T(8,128)}, f32[128,512]{1,0:T(8,128)}, f32[128,512]{1,0:T(8,128)}) custom-call(f32[64,4,128]{2,1,0:T(4,128)S(1)} %all_to_all.26.sums_ref, f32[128,512]{1,0:T(8,128)S(1)} %get-tuple-element.10.image_ref, f32[128,512]{1,0:T(8,128)S(1)} %copy-done.2, f32[128,512]{1,0:T(8,128)S(1)} %copy-done.1, f32[128,512]{1,0:T(8,128)S(1)} %copy-done), custom_call_target="tpu_custom_call" | custom-call | tf_op jit(solution)/shard_map/pallas_call | solution.py:232
  (3 shorter events, 0.1 us)
Async XLA Ops:
  1.3 7.5 %copy-start = (f32[128,512]{1,0:T(8,128)S(1)}, f32[128,512]{1,0:T(8,128)}, u32[]{:S(2)}) copy-start(f32[128,512]{1,0:T(8,128)} %direction_ref.3) | copy-start | bytes 786436
  2.9 11.6 %all-to-all-start = ((bf16[8,16,640]{2,1,0:T(8,128)(2,1)}), bf16[8,16,640]{2,1,0:T(8,128)(2,1)S(1)}, u32[]{:S(2)}, u32[]{:S(2)}) async-start(bf16[8,16,640]{2,1,0:T(8,128)(2,1)} %shard_map.94), calls=%async_computation | async-start | bytes 327680 | tf_op jit(solution)/shard_map/all_to_all | solution.py:179
  8.8 18.7 %collective-permute-start = (bf16[128,512]{1,0:T(8,128)(2,1)S(1)}, bf16[128,512]{1,0:T(8,128)(2,1)S(1)}, u32[]{:S(2)}, u32[]{:S(2)}) collective-permute-start(bf16[128,512]{1,0:T(8,128)(2,1)S(1)} %convert_element_type.3), channel_id=1, source_target_pairs={{0,2},{2,0},{1,3},{3,1},{4,6},{6,4},{5,7},{7,5},{8,10},{10,8},{9,1... | collective-permute-start | bytes 393224 | tf_op jit(solution)/shard_map/ppermute | solution.py:184
  15.3 23.0 %all-to-all-start.1 = ((bf16[16,64,128]{2,1,0:T(8,128)(2,1)}), bf16[16,64,128]{2,1,0:T(8,128)(2,1)S(1)}, u32[]{:S(2)}, u32[]{:S(2)}) async-start(bf16[16,64,128]{2,1,0:T(8,128)(2,1)} %shard_map.95), calls=%async_computation.1 | async-start | bytes 524288 | tf_op jit(solution)/shard_map/all_to_all | solution.py:179
  73.1 14.6 %copy-start.1 = (f32[128,512]{1,0:T(8,128)S(1)}, f32[128,512]{1,0:T(8,128)}, u32[]{:S(2)}) copy-start(f32[128,512]{1,0:T(8,128)} %residual_ref.3) | copy-start | bytes 786436
  73.1 14.6 %all-to-all-start.3 = ((bf16[8,128,128]{2,1,0:T(8,128)(2,1)}), bf16[8,128,128]{2,1,0:T(8,128)(2,1)S(1)}, u32[]{:S(2)}, u32[]{:S(2)}) async-start(bf16[8,128,128]{2,1,0:T(8,128)(2,1)} %shard_map.98), calls=%async_computation.3 | async-start | bytes 524288 | tf_op jit(solution)/shard_map/all_to_all | solution.py:179
  88.0 17.8 %copy-start.2 = (f32[128,512]{1,0:T(8,128)S(1)}, f32[128,512]{1,0:T(8,128)}, u32[]{:S(2)}) copy-start(f32[128,512]{1,0:T(8,128)} %solution_ref.1) | copy-start | bytes 786436
